TPU v7x, 256 devices: a whole 4x4x8 slice. The times are simulated.
256 devices in a mesh: section: 16 (over y, x), dp: 16 (over z, core).
Axes of the slice: x: 4, y: 4, z: 8, core: 2. Of those that a mesh axis runs over, the one named last changes fastest.
Arguments:
- inputs: bfloat16 [64, 32, 2304], P('dp'), may hold values from -6 to 6
- value_weight: bfloat16 [16, 2304, 2048], P('section'), may hold values from -0.25 to 0.25
- output_weight: bfloat16 [16, 2304, 2048], P('section', 'dp'), may hold values from -0.125 to 0.125
- cotangent: bfloat16 [64, 32, 2304], P('dp'), may hold values from -40 to 40
- lengths: int32 [64], P('dp'), may hold values from 8 to 32
Outputs:
- clipped_gradient: bfloat16 [16, 2304, 2048], P('section', 'dp')
All inputs are finite; a program needn't handle non-finite values.
Results may differ from a plain program's by a relative error of at most 0.03.
Values may be sent and summed in bfloat16 or wider, within the bound.
A program may use at most 128 MiB of HBM per device.

v0:
```python
import math

import jax
import jax.numpy as jnp
from jax import lax
from jax.sharding import PartitionSpec as P

EPS = 1e-06
GAMMA = 0.01


def from_behind(block, axis, distance):
    devices = range(lax.axis_size(axis))
    route = [(i - distance, i) for i in devices if i - distance in devices]
    return lax.ppermute(block, axis, route)


def contract_last(left_op, right_op):
    return lax.dot_general(
        left_op, right_op, (((1,), (1,)), ((), ())), preferred_element_type=jnp.float32
    )


def contract_first(left_op, right_op):
    return lax.dot_general(
        left_op, right_op, (((0,), (0,)), ((), ())), preferred_element_type=jnp.float32
    )


def norm_parts(hidden):
    hidden_f32 = hidden.astype(jnp.float32)
    inv_rms = lax.rsqrt(jnp.mean(hidden_f32 * hidden_f32, axis=-1, keepdims=True) + EPS)
    return (hidden_f32, inv_rms, hidden_f32 * inv_rms)


def forward_layer(hidden, w_value, w_out):
    hidden_f32, inv_rms, normed = norm_parts(hidden)
    values = jnp.dot(
        normed.astype(jnp.bfloat16), w_value, preferred_element_type=jnp.float32
    ).astype(jnp.bfloat16)
    result = (hidden_f32 + contract_last(values, w_out)).astype(jnp.bfloat16)
    return (result, values)


def backward_layer(hidden, grad_out, w_value, w_out):
    hidden_f32, inv_rms, normed = norm_parts(hidden)
    grad_values = jnp.dot(grad_out, w_out, preferred_element_type=jnp.float32).astype(jnp.bfloat16)
    grad_normed = contract_last(grad_values, w_value)
    inner_mean = jnp.mean(grad_normed * normed, axis=-1, keepdims=True)
    return (grad_out.astype(jnp.float32) + inv_rms * (grad_normed - normed * inner_mean)).astype(
        jnp.bfloat16
    )


def ghost_part(values, grad_out):
    return jnp.sum(contract_last(values, values) * contract_last(grad_out, grad_out))


def take_item(stacked, position):
    return lax.dynamic_index_in_dim(stacked, position, 0, keepdims=False)


def put_item(stacked, position, new_item, is_valid):
    old_item = take_item(stacked, position)
    return lax.dynamic_update_index_in_dim(
        stacked, jnp.where(is_valid, new_item, old_item), position, 0
    )


def per_device(inputs, value_weight, output_weight, cotangent, lengths):
    micro_count, seq_len, model_width = inputs.shape
    section_count = lax.axis_size("section")
    dp_count = lax.axis_size("dp")
    section_id = lax.axis_index("section")
    w_value = value_weight[0]
    features = w_value.shape[1]
    w_out = lax.all_gather(output_weight[0], "dp", axis=0, tiled=True)
    tick_count = micro_count + section_count - 1
    is_first = section_id == 0
    is_last = section_id == section_count - 1
    clip_scale = math.sqrt(features * model_width * 1.0 / (micro_count * dp_count))

    def live_forward(hidden_in):
        return forward_layer(hidden_in, w_value, w_out)

    def spare_forward(hidden_in):
        return (jnp.zeros_like(hidden_in), jnp.zeros((seq_len, features), jnp.bfloat16))

    def forward_tick(moment, loop_state):
        incoming, kept_hidden, kept_values = loop_state
        micro_index = moment - section_id
        is_valid = jnp.logical_and(micro_index >= 0, micro_index < micro_count)
        slot_index = jnp.clip(micro_index, 0, micro_count - 1)
        hidden = jnp.where(is_first, take_item(inputs, slot_index), incoming)
        result, values = lax.cond(is_valid, live_forward, spare_forward, hidden)
        kept_hidden = put_item(kept_hidden, slot_index, hidden, is_valid)
        kept_values = put_item(kept_values, slot_index, values, is_valid)
        passed = from_behind(result, "section", 1)
        return (passed, kept_hidden, kept_values)

    zero_state = (
        jnp.zeros((seq_len, model_width), jnp.bfloat16),
        jnp.zeros((micro_count, seq_len, model_width), jnp.bfloat16),
        jnp.zeros((micro_count, seq_len, features), jnp.bfloat16),
    )
    _, kept_hidden, kept_values = lax.fori_loop(0, tick_count, forward_tick, zero_state)
    is_live = lax.broadcasted_iota(jnp.int32, (micro_count, seq_len), 1) < lengths[:, None]
    masked = jnp.where(is_live[:, :, None], cotangent, jnp.zeros((), jnp.bfloat16))

    def live_backward(hidden_in, grad_out, values):
        return (backward_layer(hidden_in, grad_out, w_value, w_out), ghost_part(values, grad_out))

    def spare_backward(hidden_in, grad_out, values):
        return (jnp.zeros_like(grad_out), jnp.zeros((), jnp.float32))

    def backward_tick(moment, loop_state):
        incoming, kept_grads, norm_terms, weighted, grad_term = loop_state
        micro_index = moment - (section_count - 1 - section_id)
        is_valid = jnp.logical_and(micro_index >= 0, micro_index < micro_count)
        slot_index = jnp.clip(micro_index, 0, micro_count - 1)
        grad_out = jnp.where(is_last, take_item(masked, slot_index), incoming)
        hidden = take_item(kept_hidden, slot_index)
        values = take_item(kept_values, slot_index)
        grad_in, norm_part = lax.cond(
            is_valid, live_backward, spare_backward, hidden, grad_out, values
        )
        kept_grads = put_item(kept_grads, slot_index, grad_out, is_valid)
        slot_match = jnp.logical_and(is_valid, jnp.arange(micro_count) == micro_index)
        norm_terms = norm_terms + jnp.where(slot_match, norm_part, jnp.zeros((), jnp.float32))
        passed = from_behind(grad_in, "section", -1)
        return (passed, kept_grads, norm_terms, weighted, grad_term)

    term_shape = (model_width, features)
    back_state = (
        jnp.zeros((seq_len, model_width), jnp.bfloat16),
        jnp.zeros((micro_count, seq_len, model_width), jnp.bfloat16),
        jnp.zeros((micro_count,), jnp.float32),
        jnp.zeros((micro_count, seq_len, model_width), jnp.bfloat16),
        jnp.zeros(term_shape, jnp.float32),
    )
    _, kept_grads, norm_terms, weighted, grad_term = lax.fori_loop(
        0, tick_count, backward_tick, back_state
    )
    totals = lax.psum(norm_terms, "section")
    factors = clip_scale / (jnp.sqrt(totals) + GAMMA)
    weighted = (kept_grads.astype(jnp.float32) * factors[:, None, None]).astype(jnp.bfloat16)
    flat_weighted = weighted.reshape(micro_count * seq_len, model_width)
    flat_values = kept_values.reshape(micro_count * seq_len, features)
    summed = lax.psum_scatter(
        contract_first(flat_weighted, flat_values).astype(jnp.bfloat16),
        "dp",
        scatter_dimension=0,
        tiled=True,
    )
    return summed[None]


def solution(mesh):
    in_specs = (
        P("dp", None, None),
        P("section", None, None),
        P("section", "dp", None),
        P("dp", None, None),
        P("dp"),
    )
    out_specs = P("section", "dp", None)
    return jax.shard_map(
        per_device, mesh=mesh, in_specs=in_specs, out_specs=out_specs, check_vma=False
    )
```

profile of v0, /device:TPU:1, one launch (start us, length us, event | category | flops | bytes accessed | tf_op | source)
XLA Modules:
  0.0 911.0 jit_solution(10010071451447696297)
XLA Ops:
  9.2 65.1 %all-gather.3.cloned.1.call-done = bf16[1,2304,2048]{2,1,0:T(8,128)(2,1)} async-done(((bf16[1,144,2048]{2,1,0:T(8,128)(2,1)}), bf16[1,2304,2048]{2,1,0:T(8,128)(2,1)}) %all-gather.3.cloned.1.call-update) | async-done | bytes 9437200 | tf_op jit(solution)/shard_map/all_gather | solution.py:77
  74.4 259.2 %while.37 = (s32[]{:T(128)}, bf16[32,2304]{1,0:T(8,128)(2,1)S(1)}, bf16[4,32,2304]{2,1,0:T(8,128)(2,1)S(1)}, bf16[4,32,2048]{2,1,0:T(8,128)(2,1)S(1)}, s32[]{:T(...) while((s32[]{:T(128)}, bf16[32,2304]{1,0:T(8,128)(2,1)S(1)}, ...), condition=%wide.region_4.5_spmd, body=%wide.region_0.4_spmd.sunk | while | flops 604921856 | bytes 59753272 | solution.py:106
  75.4 10.2 %conditional.5 = (bf16[32,2304]{1,0:T(8,128)(2,1)S(1)}, bf16[32,2048]{1,0:T(8,128)(2,1)}) conditional(s32[]{:T(128)} %convert_element_type.91, () %tuple.94, (bf16[32,2304]{1,0:T(8,128)(2,1)S(1)}, bf16[2304,2048]{1,0:T(8,128)(2,1)}, bf16[2304,2048]{1,0:T(8,128)(2,1)}) %tuple.95), branch_computations={%region_1.1_spmd, %region_2.3_spmd} | conditional | flops 604708864 | bytes 57475628 | solution.py:95
  75.6 6.3 convolution_convert_fusion
  91.3 10.2 %conditional.5 = (bf16[32,2304]{1,0:T(8,128)(2,1)S(1)}, bf16[32,2048]{1,0:T(8,128)(2,1)}) conditional(s32[]{:T(128)} %convert_element_type.91, () %tuple.94, (bf16[32,2304]{1,0:T(8,128)(2,1)S(1)}, bf16[2304,2048]{1,0:T(8,128)(2,1)}, bf16[2304,2048]{1,0:T(8,128)(2,1)}) %tuple.95), branch_computations={%region_1.1_spmd, %region_2.3_spmd} | conditional | flops 604708864 | bytes 57475628 | solution.py:95
  91.5 6.3 convolution_convert_fusion
  109.1 10.2 %conditional.5 = (bf16[32,2304]{1,0:T(8,128)(2,1)S(1)}, bf16[32,2048]{1,0:T(8,128)(2,1)}) conditional(s32[]{:T(128)} %convert_element_type.91, () %tuple.94, (bf16[32,2304]{1,0:T(8,128)(2,1)S(1)}, bf16[2304,2048]{1,0:T(8,128)(2,1)}, bf16[2304,2048]{1,0:T(8,128)(2,1)}) %tuple.95), branch_computations={%region_1.1_spmd, %region_2.3_spmd} | conditional | flops 604708864 | bytes 57475628 | solution.py:95
  109.2 6.3 convolution_convert_fusion
  126.5 10.2 %conditional.5 = (bf16[32,2304]{1,0:T(8,128)(2,1)S(1)}, bf16[32,2048]{1,0:T(8,128)(2,1)}) conditional(s32[]{:T(128)} %convert_element_type.91, () %tuple.94, (bf16[32,2304]{1,0:T(8,128)(2,1)S(1)}, bf16[2304,2048]{1,0:T(8,128)(2,1)}, bf16[2304,2048]{1,0:T(8,128)(2,1)}) %tuple.95), branch_computations={%region_1.1_spmd, %region_2.3_spmd} | conditional | flops 604708864 | bytes 57475628 | solution.py:95
  126.7 6.3 convolution_convert_fusion
  144.3 13.4 %collective-permute-start = (bf16[32,2304]{1,0:T(8,128)(2,1)S(1)}, bf16[32,2304]{1,0:T(8,128)(2,1)S(1)}, u32[]{:S(2)}, u32[]{:S(2)}) collective-permute-start(bf16[32,2304]{1,0:T(8,128)(2,1)S(1)} %get-tuple-element.689), channel_id=1, source_target_pairs={{0,16},{16,32},{32,48},{48,64},{64,80},{80,96},{96,112},{112,128},... | collective-permute-start | bytes 442376 | tf_op jit(solution)/shard_map/while/body/eval_jaxpr/ppermute | solution.py:15
  169.0 11.8 %collective-permute-start = (bf16[32,2304]{1,0:T(8,128)(2,1)S(1)}, bf16[32,2304]{1,0:T(8,128)(2,1)S(1)}, u32[]{:S(2)}, u32[]{:S(2)}) collective-permute-start(bf16[32,2304]{1,0:T(8,128)(2,1)S(1)} %get-tuple-element.689), channel_id=1, source_target_pairs={{0,16},{16,32},{32,48},{48,64},{64,80},{80,96},{96,112},{112,128},... | collective-permute-start | bytes 442376 | tf_op jit(solution)/shard_map/while/body/eval_jaxpr/ppermute | solution.py:15
  192.3 14.1 %collective-permute-start = (bf16[32,2304]{1,0:T(8,128)(2,1)S(1)}, bf16[32,2304]{1,0:T(8,128)(2,1)S(1)}, u32[]{:S(2)}, u32[]{:S(2)}) collective-permute-start(bf16[32,2304]{1,0:T(8,128)(2,1)S(1)} %get-tuple-element.689), channel_id=1, source_target_pairs={{0,16},{16,32},{32,48},{48,64},{64,80},{80,96},{96,112},{112,128},... | collective-permute-start | bytes 442376 | tf_op jit(solution)/shard_map/while/body/eval_jaxpr/ppermute | solution.py:15
  219.8 15.5 %collective-permute-start = (bf16[32,2304]{1,0:T(8,128)(2,1)S(1)}, bf16[32,2304]{1,0:T(8,128)(2,1)S(1)}, u32[]{:S(2)}, u32[]{:S(2)}) collective-permute-start(bf16[32,2304]{1,0:T(8,128)(2,1)S(1)} %get-tuple-element.689), channel_id=1, source_target_pairs={{0,16},{16,32},{32,48},{48,64},{64,80},{80,96},{96,112},{112,128},... | collective-permute-start | bytes 442376 | tf_op jit(solution)/shard_map/while/body/eval_jaxpr/ppermute | solution.py:15
  239.0 6.2 collective-permute-start
  250.2 7.9 collective-permute-start
  261.9 7.5 collective-permute-start
  273.1 10.6 %collective-permute-start = (bf16[32,2304]{1,0:T(8,128)(2,1)S(1)}, bf16[32,2304]{1,0:T(8,128)(2,1)S(1)}, u32[]{:S(2)}, u32[]{:S(2)}) collective-permute-start(bf16[32,2304]{1,0:T(8,128)(2,1)S(1)} %get-tuple-element.689), channel_id=1, source_target_pairs={{0,16},{16,32},{32,48},{48,64},{64,80},{80,96},{96,112},{112,128},... | collective-permute-start | bytes 442376 | tf_op jit(solution)/shard_map/while/body/eval_jaxpr/ppermute | solution.py:15
  296.7 9.1 collective-permute-start
  319.6 11.9 %collective-permute-start = (bf16[32,2304]{1,0:T(8,128)(2,1)S(1)}, bf16[32,2304]{1,0:T(8,128)(2,1)S(1)}, u32[]{:S(2)}, u32[]{:S(2)}) collective-permute-start(bf16[32,2304]{1,0:T(8,128)(2,1)S(1)} %get-tuple-element.689), channel_id=1, source_target_pairs={{0,16},{16,32},{32,48},{48,64},{64,80},{80,96},{96,112},{112,128},... | collective-permute-start | bytes 442376 | tf_op jit(solution)/shard_map/while/body/eval_jaxpr/ppermute | solution.py:15
  333.6 427.5 %while.38 = (s32[]{:T(128)}, bf16[32,2304]{1,0:T(8,128)(2,1)S(1)}, bf16[4,32,2304]{2,1,0:T(8,128)(2,1)S(1)}, f32[4]{0:T(128)S(1)}, s32[]{:T(128)}, /*index=5*/pr...) while((s32[]{:T(128)}, bf16[32,2304]{1,0:T(8,128)(2,1)S(1)}, ...), condition=%wide.region_11.12_spmd.clone, body=%wide.region_5.11_spmd.clone.sunk | while | flops 614213632 | bytes 22259204 | solution.py:141
  342.2 12.4 %collective-permute-done.1 = bf16[32,2304]{1,0:T(8,128)(2,1)S(1)} collective-permute-done((bf16[32,2304]{1,0:T(8,128)(2,1)S(1)}, bf16[32,2304]{1,0:T(8,128)(2,1)S(1)}, u32[]{:S(2)}, u32[]{:S(2)}) %collective-permute-start.1) | collective-permute-done | bytes 147488 | tf_op jit(solution)/shard_map/while/body/eval_jaxpr/ppermute | solution.py:15
  356.0 6.8 collective-permute-done.1
  364.3 9.8 %collective-permute-done.1 = bf16[32,2304]{1,0:T(8,128)(2,1)S(1)} collective-permute-done((bf16[32,2304]{1,0:T(8,128)(2,1)S(1)}, bf16[32,2304]{1,0:T(8,128)(2,1)S(1)}, u32[]{:S(2)}, u32[]{:S(2)}) %collective-permute-start.1) | collective-permute-done | bytes 147488 | tf_op jit(solution)/shard_map/while/body/eval_jaxpr/ppermute | solution.py:15
  375.6 7.1 collective-permute-done.1
  384.1 8.9 collective-permute-done.1
  394.5 8.6 collective-permute-done.1
  404.5 10.9 %collective-permute-done.1 = bf16[32,2304]{1,0:T(8,128)(2,1)S(1)} collective-permute-done((bf16[32,2304]{1,0:T(8,128)(2,1)S(1)}, bf16[32,2304]{1,0:T(8,128)(2,1)S(1)}, u32[]{:S(2)}, u32[]{:S(2)}) %collective-permute-start.1) | collective-permute-done | bytes 147488 | tf_op jit(solution)/shard_map/while/body/eval_jaxpr/ppermute | solution.py:15
  416.9 8.6 collective-permute-done.1
  426.9 13.0 %collective-permute-done.1 = bf16[32,2304]{1,0:T(8,128)(2,1)S(1)} collective-permute-done((bf16[32,2304]{1,0:T(8,128)(2,1)S(1)}, bf16[32,2304]{1,0:T(8,128)(2,1)S(1)}, u32[]{:S(2)}, u32[]{:S(2)}) %collective-permute-start.1) | collective-permute-done | bytes 147488 | tf_op jit(solution)/shard_map/while/body/eval_jaxpr/ppermute | solution.py:15
  441.3 7.9 collective-permute-done.1
  450.7 11.3 %collective-permute-done.1 = bf16[32,2304]{1,0:T(8,128)(2,1)S(1)} collective-permute-done((bf16[32,2304]{1,0:T(8,128)(2,1)S(1)}, bf16[32,2304]{1,0:T(8,128)(2,1)S(1)}, u32[]{:S(2)}, u32[]{:S(2)}) %collective-permute-start.1) | collective-permute-done | bytes 147488 | tf_op jit(solution)/shard_map/while/body/eval_jaxpr/ppermute | solution.py:15
  463.5 6.8 collective-permute-done.1
  471.7 9.3 %collective-permute-done.1 = bf16[32,2304]{1,0:T(8,128)(2,1)S(1)} collective-permute-done((bf16[32,2304]{1,0:T(8,128)(2,1)S(1)}, bf16[32,2304]{1,0:T(8,128)(2,1)S(1)}, u32[]{:S(2)}, u32[]{:S(2)}) %collective-permute-start.1) | collective-permute-done | bytes 147488 | tf_op jit(solution)/shard_map/while/body/eval_jaxpr/ppermute | solution.py:15
  482.5 194.1 %collective-permute-done.1 = bf16[32,2304]{1,0:T(8,128)(2,1)S(1)} collective-permute-done((bf16[32,2304]{1,0:T(8,128)(2,1)S(1)}, bf16[32,2304]{1,0:T(8,128)(2,1)S(1)}, u32[]{:S(2)}, u32[]{:S(2)}) %collective-permute-start.1) | collective-permute-done | bytes 147488 | tf_op jit(solution)/shard_map/while/body/eval_jaxpr/ppermute | solution.py:15
  676.7 12.9 %conditional.6 = (bf16[32,2304]{1,0:T(8,128)(2,1)S(1)}, f32[]{:T(128)}) conditional(s32[]{:T(128)} %convert_element_type.92, () %tuple.98, (bf16[32,2304]{1,0:T(8,128)(2,1)S(1)}, bf16[4,32,2304]{2,1,0:T(8,128)(2,1)S(1)}, s32[]{:T(128)}, bf16[2304,2048]{1,0:T(8,128)(2,1)}, bf16[2304,2048]{1,0:T(8,128)(2,1)}, ...), branch_computations={%region_6.6_spmd, %region_7.10_spmd} | conditional | flops 614066176 | bytes 20636836 | solution.py:124
  676.8 11.0 %fusion.9 = (f32[32]{0:T(128)S(1)}, f32[32,2304]{1,0:T(8,128)S(1)}) fusion(f32[32]{0:T(128)S(1)} %add_rsqrt_fusion.1, bf16[4,32,2304]{2,1,0:T(8,128)(2,1)S(1)} %get-tuple-element.458, s32[]{:T(128)} %get-tuple-element.459, bf16[2304,2048]{1,0:T(8,128)(2,1)} %get-tuple-element.461, bf16[32,2304]{1,0:T(8,128)(2,1)S(1)} %get-tuple-element.457, ...), kind=kOutput, calls=%fused_computation.24 | convolution fusion | flops 604340224 | bytes 19464452 | tf_op jit(solution)/shard_map/while/body/eval_jaxpr/cond/branch_1_fun/dot_general | solution.py:19
  690.9 9.2 %collective-permute-done.1 = bf16[32,2304]{1,0:T(8,128)(2,1)S(1)} collective-permute-done((bf16[32,2304]{1,0:T(8,128)(2,1)S(1)}, bf16[32,2304]{1,0:T(8,128)(2,1)S(1)}, u32[]{:S(2)}, u32[]{:S(2)}) %collective-permute-start.1) | collective-permute-done | bytes 147488 | tf_op jit(solution)/shard_map/while/body/eval_jaxpr/ppermute | solution.py:15
  700.2 12.9 %conditional.6 = (bf16[32,2304]{1,0:T(8,128)(2,1)S(1)}, f32[]{:T(128)}) conditional(s32[]{:T(128)} %convert_element_type.92, () %tuple.98, (bf16[32,2304]{1,0:T(8,128)(2,1)S(1)}, bf16[4,32,2304]{2,1,0:T(8,128)(2,1)S(1)}, s32[]{:T(128)}, bf16[2304,2048]{1,0:T(8,128)(2,1)}, bf16[2304,2048]{1,0:T(8,128)(2,1)}, ...), branch_computations={%region_6.6_spmd, %region_7.10_spmd} | conditional | flops 614066176 | bytes 20636836 | solution.py:124
  700.4 11.0 %fusion.9 = (f32[32]{0:T(128)S(1)}, f32[32,2304]{1,0:T(8,128)S(1)}) fusion(f32[32]{0:T(128)S(1)} %add_rsqrt_fusion.1, bf16[4,32,2304]{2,1,0:T(8,128)(2,1)S(1)} %get-tuple-element.458, s32[]{:T(128)} %get-tuple-element.459, bf16[2304,2048]{1,0:T(8,128)(2,1)} %get-tuple-element.461, bf16[32,2304]{1,0:T(8,128)(2,1)S(1)} %get-tuple-element.457, ...), kind=kOutput, calls=%fused_computation.24 | convolution fusion | flops 604340224 | bytes 19464452 | tf_op jit(solution)/shard_map/while/body/eval_jaxpr/cond/branch_1_fun/dot_general | solution.py:19
  714.5 6.7 collective-permute-done.1
  721.3 12.9 %conditional.6 = (bf16[32,2304]{1,0:T(8,128)(2,1)S(1)}, f32[]{:T(128)}) conditional(s32[]{:T(128)} %convert_element_type.92, () %tuple.98, (bf16[32,2304]{1,0:T(8,128)(2,1)S(1)}, bf16[4,32,2304]{2,1,0:T(8,128)(2,1)S(1)}, s32[]{:T(128)}, bf16[2304,2048]{1,0:T(8,128)(2,1)}, bf16[2304,2048]{1,0:T(8,128)(2,1)}, ...), branch_computations={%region_6.6_spmd, %region_7.10_spmd} | conditional | flops 614066176 | bytes 20636836 | solution.py:124
  721.5 11.0 %fusion.9 = (f32[32]{0:T(128)S(1)}, f32[32,2304]{1,0:T(8,128)S(1)}) fusion(f32[32]{0:T(128)S(1)} %add_rsqrt_fusion.1, bf16[4,32,2304]{2,1,0:T(8,128)(2,1)S(1)} %get-tuple-element.458, s32[]{:T(128)} %get-tuple-element.459, bf16[2304,2048]{1,0:T(8,128)(2,1)} %get-tuple-element.461, bf16[32,2304]{1,0:T(8,128)(2,1)S(1)} %get-tuple-element.457, ...), kind=kOutput, calls=%fused_computation.24 | convolution fusion | flops 604340224 | bytes 19464452 | tf_op jit(solution)/shard_map/while/body/eval_jaxpr/cond/branch_1_fun/dot_general | solution.py:19
  735.5 6.7 collective-permute-done.1
  742.3 12.9 %conditional.6 = (bf16[32,2304]{1,0:T(8,128)(2,1)S(1)}, f32[]{:T(128)}) conditional(s32[]{:T(128)} %convert_element_type.92, () %tuple.98, (bf16[32,2304]{1,0:T(8,128)(2,1)S(1)}, bf16[4,32,2304]{2,1,0:T(8,128)(2,1)S(1)}, s32[]{:T(128)}, bf16[2304,2048]{1,0:T(8,128)(2,1)}, bf16[2304,2048]{1,0:T(8,128)(2,1)}, ...), branch_computations={%region_6.6_spmd, %region_7.10_spmd} | conditional | flops 614066176 | bytes 20636836 | solution.py:124
  742.5 11.0 %fusion.9 = (f32[32]{0:T(128)S(1)}, f32[32,2304]{1,0:T(8,128)S(1)}) fusion(f32[32]{0:T(128)S(1)} %add_rsqrt_fusion.1, bf16[4,32,2304]{2,1,0:T(8,128)(2,1)S(1)} %get-tuple-element.458, s32[]{:T(128)} %get-tuple-element.459, bf16[2304,2048]{1,0:T(8,128)(2,1)} %get-tuple-element.461, bf16[32,2304]{1,0:T(8,128)(2,1)S(1)} %get-tuple-element.457, ...), kind=kOutput, calls=%fused_computation.24 | convolution fusion | flops 604340224 | bytes 19464452 | tf_op jit(solution)/shard_map/while/body/eval_jaxpr/cond/branch_1_fun/dot_general | solution.py:19
  761.1 28.5 %psum.7 = f32[4]{0:T(128)S(1)} all-reduce(f32[4]{0:T(128)S(1)} %get-tuple-element.484), channel_id=1, replica_groups=mesh['section'=16,'dp'=16] {'section'}, use_global_device_ids=true, to_apply=%region_12.13 | all-reduce | flops 4 | bytes 32 | tf_op jit(solution)/shard_map/psum | solution.py:144
  794.8 109.3 %reduce-scatter.2.cloned.1.call-done = bf16[144,2048]{1,0:T(8,128)(2,1)} async-done(((bf16[2304,2048]{1,0:T(8,128)(2,1)}), bf16[144,2048]{1,0:T(8,128)(2,1)}) %reduce-scatter.2.cloned.1.call-update) | async-done | bytes 589840 | tf_op jit(solution)/shard_map/reduce_scatter | solution.py:149
  (315 shorter events, 185.9 us)
Async XLA Ops:
  6.5 67.8 %all-gather.3.cloned.1.call-start = ((), (), s32[]{:S(2)}) async-start(), calls=%async_computation.2 | async-start | bytes 10027008 | tf_op jit(solution)/shard_map/all_gather | solution.py:77
  7.3 896.9 %reduce-scatter.2.cloned.1.call-start = ((), (), s32[]{:S(2)}) async-start(), calls=%async_computation.1 | async-start | bytes 10027008 | tf_op jit(solution)/shard_map/reduce_scatter | solution.py:149
  75.5 6.4 copy-start
  85.7 4.6 collective-permute-start
  91.3 6.4 copy-start
  101.5 6.5 collective-permute-start
  109.1 6.4 copy-start
  119.3 6.2 collective-permute-start
  126.5 6.4 copy-start
  136.7 5.9 collective-permute-start
  144.3 15.4 %collective-permute-start = (bf16[32,2304]{1,0:T(8,128)(2,1)S(1)}, bf16[32,2304]{1,0:T(8,128)(2,1)S(1)}, u32[]{:S(2)}, u32[]{:S(2)}) collective-permute-start(bf16[32,2304]{1,0:T(8,128)(2,1)S(1)} %get-tuple-element.689), channel_id=1, source_target_pairs={{0,16},{16,32},{32,48},{48,64},{64,80},{80,96},{96,112},{112,128},... | collective-permute-start | bytes 442376 | tf_op jit(solution)/shard_map/while/body/eval_jaxpr/ppermute | solution.py:15
  161.5 5.9 collective-permute-start
  169.0 13.9 %collective-permute-start = (bf16[32,2304]{1,0:T(8,128)(2,1)S(1)}, bf16[32,2304]{1,0:T(8,128)(2,1)S(1)}, u32[]{:S(2)}, u32[]{:S(2)}) collective-permute-start(bf16[32,2304]{1,0:T(8,128)(2,1)S(1)} %get-tuple-element.689), channel_id=1, source_target_pairs={{0,16},{16,32},{32,48},{48,64},{64,80},{80,96},{96,112},{112,128},... | collective-permute-start | bytes 442376 | tf_op jit(solution)/shard_map/while/body/eval_jaxpr/ppermute | solution.py:15
  184.6 5.9 collective-permute-start
  192.3 16.1 %collective-permute-start = (bf16[32,2304]{1,0:T(8,128)(2,1)S(1)}, bf16[32,2304]{1,0:T(8,128)(2,1)S(1)}, u32[]{:S(2)}, u32[]{:S(2)}) collective-permute-start(bf16[32,2304]{1,0:T(8,128)(2,1)S(1)} %get-tuple-element.689), channel_id=1, source_target_pairs={{0,16},{16,32},{32,48},{48,64},{64,80},{80,96},{96,112},{112,128},... | collective-permute-start | bytes 442376 | tf_op jit(solution)/shard_map/while/body/eval_jaxpr/ppermute | solution.py:15
  210.1 8.0 collective-permute-start
  219.8 17.5 %collective-permute-start = (bf16[32,2304]{1,0:T(8,128)(2,1)S(1)}, bf16[32,2304]{1,0:T(8,128)(2,1)S(1)}, u32[]{:S(2)}, u32[]{:S(2)}) collective-permute-start(bf16[32,2304]{1,0:T(8,128)(2,1)S(1)} %get-tuple-element.689), channel_id=1, source_target_pairs={{0,16},{16,32},{32,48},{48,64},{64,80},{80,96},{96,112},{112,128},... | collective-permute-start | bytes 442376 | tf_op jit(solution)/shard_map/while/body/eval_jaxpr/ppermute | solution.py:15
  239.0 9.5 %collective-permute-start = (bf16[32,2304]{1,0:T(8,128)(2,1)S(1)}, bf16[32,2304]{1,0:T(8,128)(2,1)S(1)}, u32[]{:S(2)}, u32[]{:S(2)}) collective-permute-start(bf16[32,2304]{1,0:T(8,128)(2,1)S(1)} %get-tuple-element.689), channel_id=1, source_target_pairs={{0,16},{16,32},{32,48},{48,64},{64,80},{80,96},{96,112},{112,128},... | collective-permute-start | bytes 442376 | tf_op jit(solution)/shard_map/while/body/eval_jaxpr/ppermute | solution.py:15
  250.2 10.0 %collective-permute-start = (bf16[32,2304]{1,0:T(8,128)(2,1)S(1)}, bf16[32,2304]{1,0:T(8,128)(2,1)S(1)}, u32[]{:S(2)}, u32[]{:S(2)}) collective-permute-start(bf16[32,2304]{1,0:T(8,128)(2,1)S(1)} %get-tuple-element.689), channel_id=1, source_target_pairs={{0,16},{16,32},{32,48},{48,64},{64,80},{80,96},{96,112},{112,128},... | collective-permute-start | bytes 442376 | tf_op jit(solution)/shard_map/while/body/eval_jaxpr/ppermute | solution.py:15
  261.9 9.5 %collective-permute-start = (bf16[32,2304]{1,0:T(8,128)(2,1)S(1)}, bf16[32,2304]{1,0:T(8,128)(2,1)S(1)}, u32[]{:S(2)}, u32[]{:S(2)}) collective-permute-start(bf16[32,2304]{1,0:T(8,128)(2,1)S(1)} %get-tuple-element.689), channel_id=1, source_target_pairs={{0,16},{16,32},{32,48},{48,64},{64,80},{80,96},{96,112},{112,128},... | collective-permute-start | bytes 442376 | tf_op jit(solution)/shard_map/while/body/eval_jaxpr/ppermute | solution.py:15
  273.1 12.7 %collective-permute-start = (bf16[32,2304]{1,0:T(8,128)(2,1)S(1)}, bf16[32,2304]{1,0:T(8,128)(2,1)S(1)}, u32[]{:S(2)}, u32[]{:S(2)}) collective-permute-start(bf16[32,2304]{1,0:T(8,128)(2,1)S(1)} %get-tuple-element.689), channel_id=1, source_target_pairs={{0,16},{16,32},{32,48},{48,64},{64,80},{80,96},{96,112},{112,128},... | collective-permute-start | bytes 442376 | tf_op jit(solution)/shard_map/while/body/eval_jaxpr/ppermute | solution.py:15
  287.5 7.5 collective-permute-start
  296.7 11.2 %collective-permute-start = (bf16[32,2304]{1,0:T(8,128)(2,1)S(1)}, bf16[32,2304]{1,0:T(8,128)(2,1)S(1)}, u32[]{:S(2)}, u32[]{:S(2)}) collective-permute-start(bf16[32,2304]{1,0:T(8,128)(2,1)S(1)} %get-tuple-element.689), channel_id=1, source_target_pairs={{0,16},{16,32},{32,48},{48,64},{64,80},{80,96},{96,112},{112,128},... | collective-permute-start | bytes 442376 | tf_op jit(solution)/shard_map/while/body/eval_jaxpr/ppermute | solution.py:15
  309.6 8.3 collective-permute-start
  319.6 14.0 %collective-permute-start = (bf16[32,2304]{1,0:T(8,128)(2,1)S(1)}, bf16[32,2304]{1,0:T(8,128)(2,1)S(1)}, u32[]{:S(2)}, u32[]{:S(2)}) collective-permute-start(bf16[32,2304]{1,0:T(8,128)(2,1)S(1)} %get-tuple-element.689), channel_id=1, source_target_pairs={{0,16},{16,32},{32,48},{48,64},{64,80},{80,96},{96,112},{112,128},... | collective-permute-start | bytes 442376 | tf_op jit(solution)/shard_map/while/body/eval_jaxpr/ppermute | solution.py:15
  333.8 6.9 collective-permute-start.1
  340.9 13.7 %collective-permute-start.1 = (bf16[32,2304]{1,0:T(8,128)(2,1)S(1)}, bf16[32,2304]{1,0:T(8,128)(2,1)S(1)}, u32[]{:S(2)}, u32[]{:S(2)}) collective-permute-start(bf16[32,2304]{1,0:T(8,128)(2,1)S(1)} %get-tuple-element.704), channel_id=1, source_target_pairs={{16,0},{32,16},{48,32},{64,48},{80,64},{96,80},{112,96},{128,112},... | collective-permute-start | bytes 442376 | tf_op jit(solution)/shard_map/while/body/eval_jaxpr/ppermute | solution.py:15
  354.7 8.1 collective-permute-start.1
  363.0 11.2 %collective-permute-start.1 = (bf16[32,2304]{1,0:T(8,128)(2,1)S(1)}, bf16[32,2304]{1,0:T(8,128)(2,1)S(1)}, u32[]{:S(2)}, u32[]{:S(2)}) collective-permute-start(bf16[32,2304]{1,0:T(8,128)(2,1)S(1)} %get-tuple-element.704), channel_id=1, source_target_pairs={{16,0},{32,16},{48,32},{64,48},{80,64},{96,80},{112,96},{128,112},... | collective-permute-start | bytes 442376 | tf_op jit(solution)/shard_map/while/body/eval_jaxpr/ppermute | solution.py:15
  374.3 8.4 collective-permute-start.1
  382.8 10.3 %collective-permute-start.1 = (bf16[32,2304]{1,0:T(8,128)(2,1)S(1)}, bf16[32,2304]{1,0:T(8,128)(2,1)S(1)}, u32[]{:S(2)}, u32[]{:S(2)}) collective-permute-start(bf16[32,2304]{1,0:T(8,128)(2,1)S(1)} %get-tuple-element.704), channel_id=1, source_target_pairs={{16,0},{32,16},{48,32},{64,48},{80,64},{96,80},{112,96},{128,112},... | collective-permute-start | bytes 442376 | tf_op jit(solution)/shard_map/while/body/eval_jaxpr/ppermute | solution.py:15
  393.2 9.9 %collective-permute-start.1 = (bf16[32,2304]{1,0:T(8,128)(2,1)S(1)}, bf16[32,2304]{1,0:T(8,128)(2,1)S(1)}, u32[]{:S(2)}, u32[]{:S(2)}) collective-permute-start(bf16[32,2304]{1,0:T(8,128)(2,1)S(1)} %get-tuple-element.704), channel_id=1, source_target_pairs={{16,0},{32,16},{48,32},{64,48},{80,64},{96,80},{112,96},{128,112},... | collective-permute-start | bytes 442376 | tf_op jit(solution)/shard_map/while/body/eval_jaxpr/ppermute | solution.py:15
  403.2 12.2 %collective-permute-start.1 = (bf16[32,2304]{1,0:T(8,128)(2,1)S(1)}, bf16[32,2304]{1,0:T(8,128)(2,1)S(1)}, u32[]{:S(2)}, u32[]{:S(2)}) collective-permute-start(bf16[32,2304]{1,0:T(8,128)(2,1)S(1)} %get-tuple-element.704), channel_id=1, source_target_pairs={{16,0},{32,16},{48,32},{64,48},{80,64},{96,80},{112,96},{128,112},... | collective-permute-start | bytes 442376 | tf_op jit(solution)/shard_map/while/body/eval_jaxpr/ppermute | solution.py:15
  415.5 9.9 %collective-permute-start.1 = (bf16[32,2304]{1,0:T(8,128)(2,1)S(1)}, bf16[32,2304]{1,0:T(8,128)(2,1)S(1)}, u32[]{:S(2)}, u32[]{:S(2)}) collective-permute-start(bf16[32,2304]{1,0:T(8,128)(2,1)S(1)} %get-tuple-element.704), channel_id=1, source_target_pairs={{16,0},{32,16},{48,32},{64,48},{80,64},{96,80},{112,96},{128,112},... | collective-permute-start | bytes 442376 | tf_op jit(solution)/shard_map/while/body/eval_jaxpr/ppermute | solution.py:15
  425.6 14.3 %collective-permute-start.1 = (bf16[32,2304]{1,0:T(8,128)(2,1)S(1)}, bf16[32,2304]{1,0:T(8,128)(2,1)S(1)}, u32[]{:S(2)}, u32[]{:S(2)}) collective-permute-start(bf16[32,2304]{1,0:T(8,128)(2,1)S(1)} %get-tuple-element.704), channel_id=1, source_target_pairs={{16,0},{32,16},{48,32},{64,48},{80,64},{96,80},{112,96},{128,112},... | collective-permute-start | bytes 442376 | tf_op jit(solution)/shard_map/while/body/eval_jaxpr/ppermute | solution.py:15
  440.0 9.2 %collective-permute-start.1 = (bf16[32,2304]{1,0:T(8,128)(2,1)S(1)}, bf16[32,2304]{1,0:T(8,128)(2,1)S(1)}, u32[]{:S(2)}, u32[]{:S(2)}) collective-permute-start(bf16[32,2304]{1,0:T(8,128)(2,1)S(1)} %get-tuple-element.704), channel_id=1, source_target_pairs={{16,0},{32,16},{48,32},{64,48},{80,64},{96,80},{112,96},{128,112},... | collective-permute-start | bytes 442376 | tf_op jit(solution)/shard_map/while/body/eval_jaxpr/ppermute | solution.py:15
  449.4 12.7 %collective-permute-start.1 = (bf16[32,2304]{1,0:T(8,128)(2,1)S(1)}, bf16[32,2304]{1,0:T(8,128)(2,1)S(1)}, u32[]{:S(2)}, u32[]{:S(2)}) collective-permute-start(bf16[32,2304]{1,0:T(8,128)(2,1)S(1)} %get-tuple-element.704), channel_id=1, source_target_pairs={{16,0},{32,16},{48,32},{64,48},{80,64},{96,80},{112,96},{128,112},... | collective-permute-start | bytes 442376 | tf_op jit(solution)/shard_map/while/body/eval_jaxpr/ppermute | solution.py:15
  462.2 8.1 collective-permute-start.1
  470.4 10.6 %collective-permute-start.1 = (bf16[32,2304]{1,0:T(8,128)(2,1)S(1)}, bf16[32,2304]{1,0:T(8,128)(2,1)S(1)}, u32[]{:S(2)}, u32[]{:S(2)}) collective-permute-start(bf16[32,2304]{1,0:T(8,128)(2,1)S(1)} %get-tuple-element.704), channel_id=1, source_target_pairs={{16,0},{32,16},{48,32},{64,48},{80,64},{96,80},{112,96},{128,112},... | collective-permute-start | bytes 442376 | tf_op jit(solution)/shard_map/while/body/eval_jaxpr/ppermute | solution.py:15
  481.2 195.4 %collective-permute-start.1 = (bf16[32,2304]{1,0:T(8,128)(2,1)S(1)}, bf16[32,2304]{1,0:T(8,128)(2,1)S(1)}, u32[]{:S(2)}, u32[]{:S(2)}) collective-permute-start(bf16[32,2304]{1,0:T(8,128)(2,1)S(1)} %get-tuple-element.704), channel_id=1, source_target_pairs={{16,0},{32,16},{48,32},{64,48},{80,64},{96,80},{112,96},{128,112},... | collective-permute-start | bytes 442376 | tf_op jit(solution)/shard_map/while/body/eval_jaxpr/ppermute | solution.py:15
  689.6 10.5 %collective-permute-start.1 = (bf16[32,2304]{1,0:T(8,128)(2,1)S(1)}, bf16[32,2304]{1,0:T(8,128)(2,1)S(1)}, u32[]{:S(2)}, u32[]{:S(2)}) collective-permute-start(bf16[32,2304]{1,0:T(8,128)(2,1)S(1)} %get-tuple-element.704), channel_id=1, source_target_pairs={{16,0},{32,16},{48,32},{64,48},{80,64},{96,80},{112,96},{128,112},... | collective-permute-start | bytes 442376 | tf_op jit(solution)/shard_map/while/body/eval_jaxpr/ppermute | solution.py:15
  713.2 8.0 collective-permute-start.1
  734.2 8.0 collective-permute-start.1
  755.3 5.9 collective-permute-start.1
Sparse Core Ops, SparseCore 0:
  9.2 65.0 all-gather.2
  794.9 109.1 reduce-scatter.1
where the time goes:
time: 915 us; the launch traced here: 911 us
  waiting for transfers between devices  560 us (61%)
  starting transfers between devices  171 us (19%)
  matrix products  93.3 us (10%)
  blocking collectives  28.5 us (3%)
  other arithmetic  28.4 us (3%)
  between operations  13.5 us (1%)
  local copies, waits for them, and re-layouts  11.3 us (1%)
    ppermute x38, waiting for transfers between devices, from_behind(): return lax.ppermute(block, axis, route)  385 us
    ppermute x38, starting transfers between devices, from_behind(): return lax.ppermute(block, axis, route)  171 us
    reduce_scatter x1, waiting for transfers between devices, per_device(): lax.psum_scatter(contract_first(flat_weighted, flat_values).astype(jnp.bf...  109 us
    all_gather x1, waiting for transfers between devices, per_device(): w_out = lax.all_gather(output_weight[0], 'dp', axis=0, tiled=True)  65.1 us
    dot_general x16, matrix products, contract_last(): lax.dot_general(left_op, right_op, (((1,), (1,)), ((), ())), preferred_el...  63 us
    psum x1, blocking collectives, per_device(): totals = lax.psum(norm_terms, 'section')  28.5 us
    dot_general x4, matrix products, forward_layer(): jnp.dot(normed.astype(jnp.bfloat16), w_value, preferred_element_type=jnp....  25.1 us
    dynamic_update_slice x57, other arithmetic, put_item(): lax.dynamic_update_index_in_dim(stacked, jnp.where(is_valid, new_item, ol...  24.3 us
  transfers between devices with their start and end apart: 40, of which 40 were waited for; matrix products, arithmetic and copies ran while one was open for 1% of the time, Pallas kernels for 0%

commit v1 on v0

v1 whole, which is shorter than its diff:
```python
import functools
import math

import jax
import jax.numpy as jnp
from jax import lax
from jax.experimental import pallas as pl
from jax.experimental.pallas import tpu as pltpu
from jax.sharding import PartitionSpec as P

EPS = 1e-06
GAMMA = 0.01
MESH = pl.DeviceIdType.MESH
F32 = jnp.float32
BF16 = jnp.bfloat16


def dot_nn(a, b):
    return lax.dot_general(a, b, (((1,), (0,)), ((), ())), preferred_element_type=F32)


def dot_nt(a, b):
    return lax.dot_general(a, b, (((1,), (1,)), ((), ())), preferred_element_type=F32)


def dot_tn(a, b):
    return lax.dot_general(a, b, (((0,), (0,)), ((), ())), preferred_element_type=F32)


def pick(cond, fn):
    def run():
        fn()

    pl.when(cond)(run)


def relay_kernel(
    cfg, inp_ref, value_ref, slice_ref, cot_ref, len_ref, hk_ref, gk_ref,
    vbuf, wbuf, pbuf, tbuf, hbuf, obuf, gbuf, qbuf, ubuf,
    load_sem, sib_sem, ring_send, ring_recv, h_send, h_recv, g_send, g_recv,
    keep_send, keep_recv,
):
    secs, chips, per, width, cw, nch, tsec = cfg
    half_ring = chips // 2
    rows_sl = slice_ref.shape[0]
    count = 2 * per
    cn = width // nch
    sec = lax.axis_index("section")
    dp = lax.axis_index("dp")
    chip = lax.div(dp, 2)
    core = lax.rem(dp, 2)
    sib = (sec, dp + 1 - 2 * core)
    up = (sec, lax.rem(chip + 1, chips) * 2 + core)
    down = (sec, lax.rem(chip + chips - 1, chips) * 2 + core)
    nxt = (lax.rem(sec + 1, secs), dp)
    prv = (lax.rem(sec + secs - 1, secs), dp)
    first, last = sec == 0, sec == secs - 1

    barrier = pltpu.get_barrier_semaphore()
    for dev in (sib, up, down, nxt, prv):
        pl.semaphore_signal(barrier, inc=1, device_id=dev, device_id_type=MESH)
    pl.semaphore_wait(barrier, 5)

    def remote(src, dst, send, recv, dev):
        return pltpu.make_async_remote_copy(
            src_ref=src, dst_ref=dst, send_sem=send, recv_sem=recv, device_id=dev, device_id_type=MESH
        )

    def slice_rows(index):
        return wbuf.at[pl.ds(pl.multiple_of(index * rows_sl, 16), rows_sl), :]

    def mask_rows(slot, position):
        seq = gbuf.shape[1]
        live = lax.broadcasted_iota(jnp.int32, (seq, 1), 0) < len_ref[position]
        gbuf[slot] = jnp.where(live, gbuf[slot].astype(F32), 0.0).astype(BF16)

    def keep(src, dst_ref, kind, mb):
        def far():
            remote(src, dst_ref.at[mb], keep_send.at[kind, mb], keep_recv.at[kind, mb], sib).start()

        def near():
            pltpu.make_async_copy(src, dst_ref.at[mb - per], keep_send.at[kind, mb]).start()

        pick(mb < per, far)
        pick(mb >= per, near)

    def helper_core():
        to_sib = remote(slice_ref, slice_rows(2 * chip), sib_sem.at[0], sib_sem.at[1], sib)
        to_sib.start()

        def send_inputs():
            for i in range(per):
                remote(inp_ref.at[i], hbuf.at[i], h_send.at[i], h_recv.at[i], sib).start()
            for i in range(per):
                remote(inp_ref.at[i], hbuf.at[i], h_send.at[i], h_recv.at[i], sib).wait_send()

        def send_cot():
            for i in range(per):
                pltpu.make_async_copy(cot_ref.at[i], gbuf.at[i], load_sem.at[i]).start()
            for i in range(per):
                pltpu.make_async_copy(cot_ref.at[i], gbuf.at[i], load_sem.at[i]).wait()
                mask_rows(i, i)
                remote(gbuf.at[i], gbuf.at[i], g_send.at[i], g_recv.at[i], sib).start()
            for i in range(per):
                remote(gbuf.at[i], gbuf.at[i], g_send.at[i], g_recv.at[i], sib).wait_send()

        pick(first, send_inputs)
        pick(last, send_cot)
        to_sib.wait_send()
        for i in range(per):
            remote(hbuf.at[i], hk_ref.at[i], keep_send.at[0, i], keep_recv.at[0, i], sib).wait_recv()
            remote(gbuf.at[i], gk_ref.at[i], keep_send.at[1, i], keep_recv.at[1, i], sib).wait_recv()

    def relay_core():
        load_v = pltpu.make_async_copy(value_ref, vbuf, load_sem.at[0])
        load_w = pltpu.make_async_copy(slice_ref, slice_rows(2 * chip + 1), load_sem.at[1])
        load_in = pltpu.make_async_copy(inp_ref, hbuf.at[pl.ds(per, per)], load_sem.at[2])
        load_cot = pltpu.make_async_copy(cot_ref, gbuf.at[pl.ds(per, per)], load_sem.at[3])

        def ring(way, dist, half, src=None):
            step = dist - 1
            origin = lax.rem(chip + chips - step, chips) if way == 0 else lax.rem(chip + step, chips)
            block = slice_rows(2 * origin + half)
            dev = up if way == 0 else down
            return remote(
                block if src is None else src, block,
                ring_send.at[way, step, half], ring_recv.at[way, step, half], dev,
            )

        def arrived(way, dist, half):
            origin = lax.rem(chip + chips - dist, chips) if way == 0 else lax.rem(chip + dist, chips)
            block = slice_rows(2 * origin + half)
            remote(
                block, block, ring_send.at[way, dist - 1, half], ring_recv.at[way, dist - 1, half], up
            ).wait_recv()

        for way in range(2):
            ring(way, 1, 1, slice_ref).start()
        load_w.start()
        load_v.start()
        pick(first, load_in.start)
        pick(last, load_cot.start)
        remote(slice_ref, slice_rows(2 * chip), sib_sem.at[0], sib_sem.at[1], sib).wait_recv()
        for way in range(2):
            ring(way, 1, 0).start()
        pick(first, load_in.wait)

        def ready_cot():
            load_cot.wait()
            for i in range(per):
                mask_rows(per + i, i)

        pick(last, ready_cot)
        load_w.wait()
        load_v.wait()

        def slice_event(index):
            gap = lax.rem(lax.div(index, 2) + chips - chip, chips)
            dist = jnp.minimum(gap, chips - gap)
            near = 2 * dist - lax.rem(index, 2)
            return jnp.where(dist == 0, 0, jnp.where(dist == half_ring, 2 * half_ring - 1, near))

        def chunk_event(j):
            lo, hi = lax.div(cw * j, rows_sl), lax.div(cw * j + cw - 1, rows_sl)
            event = slice_event(lo)
            for extra in range(1, cw // rows_sl + 2):
                event = jnp.maximum(event, slice_event(jnp.minimum(lo + extra, hi)))
            return event

        def make_p(event):
            def chunk(j, _):
                def run():
                    off = pl.multiple_of(j * cw, cw)
                    for m in range(nch):
                        block = dot_nt(vbuf[m * cn:(m + 1) * cn, :], wbuf[pl.ds(off, cw), :])
                        pbuf[m * cn:(m + 1) * cn, pl.ds(off, cw)] = block.astype(BF16)

                pick(chunk_event(j) == event, run)
                return 0

            lax.fori_loop(0, width // cw, chunk, 0)

        def ring_event(e, _):
            dist, half = lax.div(e + 1, 2), lax.rem(e, 2)

            def turn():
                arrived(0, dist, half)
                pick(jnp.logical_or(dist + 1 < half_ring, half == 0), ring(0, dist + 1, half).start)
                arrived(1, dist, half)
                pick(jnp.logical_or(dist + 1 < half_ring, half == 1), ring(1, dist + 1, half).start)

            def final():
                arrived(0, half_ring, 0)
                arrived(1, half_ring, 1)

            pick(jnp.logical_and(e > 0, e < 2 * half_ring - 1), turn)
            pick(e == 2 * half_ring - 1, final)
            make_p(e)
            return 0

        lax.fori_loop(0, 2 * half_ring, ring_event, 0)

        def make_t():
            def chunk(j, _):
                off = pl.multiple_of(j * cw, cw)
                for m in range(nch):
                    block = dot_nt(wbuf[pl.ds(off, cw), :], vbuf[m * cn:(m + 1) * cn, :])
                    tbuf[pl.ds(off, cw), m * cn:(m + 1) * cn] = block.astype(BF16)
                return 0

            lax.fori_loop(0, width // cw, chunk, 0)

        pick(sec >= tsec, make_t)

        def whole(buf, mb, send, recv, dev):
            return remote(buf.at[mb], buf.at[mb], send.at[mb], recv.at[mb], dev)

        def inv_rms(h32):
            return lax.rsqrt(jnp.mean(h32 * h32, axis=-1, keepdims=True) + EPS)

        def forward(mb, _):
            pick(jnp.logical_or(sec > 0, mb < per), whole(hbuf, mb, h_send, h_recv, sib).wait_recv)
            keep(hbuf.at[mb], hk_ref, 0, mb)
            h = hbuf[mb]
            h32 = h.astype(F32)
            r = inv_rms(h32)
            for c in range(nch):
                cols = pl.ds(c * cn, cn)
                u = dot_nn(h, pbuf[:, c * cn:(c + 1) * cn])
                ubuf[mb, :, c * cn:(c + 1) * cn] = u
                obuf[mb, :, c * cn:(c + 1) * cn] = (h32[:, c * cn:(c + 1) * cn] + r * u).astype(BF16)
                remote(
                    obuf.at[mb, :, cols], hbuf.at[mb, :, cols], h_send.at[mb], h_recv.at[mb], nxt
                ).start()
            return 0

        pick(sec < secs - 1, lambda: lax.fori_loop(0, count, forward, 0))
        pick(jnp.logical_and(sec > 0, sec < tsec), make_t)

        def send_grad(mb, c):
            cols = pl.ds(c * cn, cn)
            remote(
                qbuf.at[mb, :, cols], gbuf.at[mb, :, cols], g_send.at[mb], g_recv.at[mb], prv
            ).start()

        def backward(mb, _):
            whole(gbuf, mb, g_send, g_recv, sib).wait_recv()
            keep(gbuf.at[mb], gk_ref, 1, mb)
            g = gbuf[mb]
            g32, h32 = g.astype(F32), hbuf[mb].astype(F32)
            r = inv_rms(h32)
            coef = jnp.sum(g32 * ubuf[mb], axis=-1, keepdims=True) * (r * r * r) * (1.0 / width)
            for c in range(nch):
                lo, hi = c * cn, (c + 1) * cn
                p = dot_nn(g, tbuf[:, lo:hi])
                qbuf[mb, :, lo:hi] = (g32[:, lo:hi] + r * p - coef * h32[:, lo:hi]).astype(BF16)
                send_grad(mb, c)
            return 0

        def backward_last(mb, _):
            pick(mb < per, whole(gbuf, mb, g_send, g_recv, sib).wait_recv)
            keep(gbuf.at[mb], gk_ref, 1, mb)
            whole(hbuf, mb, h_send, h_recv, sib).wait_recv()
            keep(hbuf.at[mb], hk_ref, 0, mb)
            g = gbuf[mb]
            g32, h32 = g.astype(F32), hbuf[mb].astype(F32)
            r = inv_rms(h32)
            dots = jnp.zeros_like(r)
            for c in range(nch):
                lo, hi = c * cn, (c + 1) * cn
                p = dot_nn(g, tbuf[:, lo:hi])
                ubuf[mb, :, lo:hi] = p
                dots = dots + jnp.sum(p * h32[:, lo:hi], axis=-1, keepdims=True)
            coef = dots * (r * r * r) * (1.0 / width)
            for c in range(nch):
                lo, hi = c * cn, (c + 1) * cn
                p = ubuf[mb, :, lo:hi]
                qbuf[mb, :, lo:hi] = (g32[:, lo:hi] + r * p - coef * h32[:, lo:hi]).astype(BF16)
                send_grad(mb, c)
            return 0

        def backward_first(mb, _):
            whole(gbuf, mb, g_send, g_recv, sib).wait_recv()
            keep(gbuf.at[mb], gk_ref, 1, mb)
            return 0

        pick(last, lambda: lax.fori_loop(0, count, backward_last, 0))
        pick(
            jnp.logical_and(sec > 0, sec < secs - 1),
            lambda: lax.fori_loop(0, count, backward, 0),
        )
        pick(first, lambda: lax.fori_loop(0, count, backward_first, 0))

        def drain(mb, _):
            pick(sec < secs - 1, whole(hbuf, mb, h_send, h_recv, nxt).wait_send)
            pick(sec > 0, whole(gbuf, mb, g_send, g_recv, prv).wait_send)
            for kind, buf, out in ((0, hbuf, hk_ref), (1, gbuf, gk_ref)):
                pick(mb < per, remote(buf.at[mb], out.at[0], keep_send.at[kind, mb], keep_recv.at[kind, mb], sib).wait_send)
                pick(mb >= per, pltpu.make_async_copy(buf.at[mb], out.at[0], keep_send.at[kind, mb]).wait)
            return 0

        lax.fori_loop(0, count, drain, 0)
        for way in range(2):
            for dist in range(1, half_ring + 1):
                for half in range(2):
                    if dist < half_ring or half == way:
                        ring(way, dist, half).wait_send()

    pick(core == 0, helper_core)
    pick(core == 1, relay_core)


def relay(inputs, value_weight, output_weight, cotangent, lengths, cw, nch, tsec):
    per, seq, width = inputs.shape
    features = value_weight.shape[1]
    secs, chips = lax.axis_size("section"), lax.axis_size("dp") // 2
    count = 2 * per
    any_spec = pl.BlockSpec(memory_space=pl.ANY)
    keep = jax.ShapeDtypeStruct((per, seq, width), BF16)
    dma = pltpu.SemaphoreType.DMA
    return pl.pallas_call(
        functools.partial(relay_kernel, (secs, chips, per, width, cw, nch, tsec)),
        out_shape=(keep, keep),
        in_specs=[any_spec] * 4 + [pl.BlockSpec(memory_space=pltpu.SMEM)],
        out_specs=(any_spec, any_spec),
        scratch_shapes=[
            pltpu.VMEM((width, features), BF16),
            pltpu.VMEM((width, features), BF16),
            pltpu.VMEM((width, width), BF16),
            pltpu.VMEM((width, width), BF16),
            pltpu.VMEM((count, seq, width), BF16),
            pltpu.VMEM((count, seq, width), BF16),
            pltpu.VMEM((count, seq, width), BF16),
            pltpu.VMEM((count, seq, width), BF16),
            pltpu.VMEM((count, seq, width), F32),
            dma((per + 4,)),
            dma((2,)),
            dma((2, chips // 2, 2)),
            dma((2, chips // 2, 2)),
            dma((count,)),
            dma((count,)),
            dma((count,)),
            dma((count,)),
            dma((2, count)),
            dma((2, count)),
        ],
        compiler_params=pltpu.CompilerParams(
            collective_id=0, has_side_effects=True, vmem_limit_bytes=60 << 20
        ),
    )(inputs, value_weight, output_weight, cotangent, lengths)


def per_device(inputs, value_weight, output_weight, cotangent, lengths, cw=256, nch=3, tsec=10):
    per, seq, width = inputs.shape
    w_value = value_weight[0]
    features = w_value.shape[1]
    clip_scale = math.sqrt(features * width * 1.0 / (per * lax.axis_size("dp")))
    hidden, grads = relay(inputs, w_value, output_weight[0], cotangent, lengths, cw, nch, tsec)
    h32 = hidden.astype(F32)
    normed = (h32 * lax.rsqrt(jnp.mean(h32 * h32, axis=-1, keepdims=True) + EPS)).astype(BF16)
    values = dot_nn(normed.reshape(per * seq, width), w_value).astype(BF16)
    v3 = values.reshape(per, seq, features)
    gram_v = jnp.einsum("etf,esf->ets", v3, v3, preferred_element_type=F32)
    gram_g = jnp.einsum("etc,esc->ets", grads, grads, preferred_element_type=F32)
    totals = lax.psum(jnp.sum(gram_v * gram_g, axis=(1, 2)), "section")
    factors = clip_scale / (jnp.sqrt(totals) + GAMMA)
    weighted = (grads.astype(F32) * factors[:, None, None]).astype(BF16)
    summed = lax.psum_scatter(
        dot_tn(weighted.reshape(per * seq, width), values).astype(BF16), "dp", scatter_dimension=0, tiled=True
    )
    return summed[None]


def solution(mesh):
    in_specs = (
        P("dp", None, None), P("section", None, None), P("section", "dp", None), P("dp", None, None), P("dp"),
    )
    return jax.shard_map(
        per_device, mesh=mesh, in_specs=in_specs, out_specs=P("section", "dp", None), check_vma=False
    )
```

time: 915 us -> 358 us (0.39)
  waiting for transfers between devices: 560 us -> 62.5 us
  Pallas kernels: 0 us -> 237 us
  starting transfers between devices: 171 us -> 0.01 us
  matrix products: 93.3 us -> 10.9 us
  other arithmetic: 28.4 us -> 2.69 us
  local copies, waits for them, and re-layouts: 11.3 us -> 0.01 us
    ppermute x38 -> x0, waiting for transfers between devices: 385 us -> none  [from_behind(): return lax.ppermute(block, axis, route)]
    pallas_call x0 -> x1, Pallas kernels: none -> 237 us  [relay(): pl.pallas_call(functools.partial(relay_kernel, (secs, chips, per, width,...]
    ppermute x38 -> x0, starting transfers between devices: 171 us -> none  [from_behind(): return lax.ppermute(block, axis, route)]
    dot_general x21 -> x4, matrix products: 93.3 us -> 10.9 us  [the longest x1 5.21 us: dot_nn(): lax.dot_general(a, b, (((1,), (0,)), ((), ())), preferred_element_type=F32)]
    all_gather x1 -> x0, waiting for transfers between devices: 65.1 us -> none  [per_device(): w_out = lax.all_gather(output_weight[0], 'dp', axis=0, tiled=True)]
    reduce_scatter x1, waiting for transfers between devices: 109 us -> 62.5 us  [per_device(): lax.psum_scatter(dot_tn(weighted.reshape(per * seq, width), values).astyp...]
    dynamic_update_slice x57 -> x0, other arithmetic: 24.3 us -> none  [put_item(): lax.dynamic_update_index_in_dim(stacked, jnp.where(is_valid, new_item, ol...]
    another operation x49 -> x0, local copies, waits for them, and re-layouts: 10.5 us -> none
  transfers between devices with their start and end apart: 40 -> 1, of which waited for: 40 -> 1; matrix products, arithmetic and copies ran while one was open for 1% -> 0% of each run, Pallas kernels for 0% -> 0%
where the time goes in v1:
time: 358 us; the launch traced here: 356 us
  Pallas kernels  237 us (66%)
  waiting for transfers between devices  62.5 us (17%)
  blocking collectives  28.7 us (8%)
  between operations  13.4 us (4%)
  matrix products  10.9 us (3%)
    pallas_call x1, Pallas kernels, relay(): pl.pallas_call(functools.partial(relay_kernel, (secs, chips, per, width,...  237 us
    reduce_scatter x1, waiting for transfers between devices, per_device(): lax.psum_scatter(dot_tn(weighted.reshape(per * seq, width), values).astyp...  62.5 us
    psum x1, blocking collectives, per_device(): totals = lax.psum(jnp.sum(gram_v * gram_g, axis=(1, 2)), 'section')  28.7 us
  transfers between devices with their start and end apart: 1, of which 1 were waited for; matrix products, arithmetic and copies ran while one was open for 0% of the time, Pallas kernels for 0%

profile of v1, /device:TPU:1, one launch (start us, length us, event | category | flops | bytes accessed | tf_op | source)
XLA Modules:
  0.0 355.6 jit_solution(18410378153261520101)
XLA Ops:
  6.5 0.0 reduce-scatter.2.cloned.1.call-start
  6.5 237.3 %shard_map.55 = (bf16[4,32,2304]{2,1,0:T(8,128)(2,1)}, bf16[4,32,2304]{2,1,0:T(8,128)(2,1)}) custom-call(bf16[4,32,2304]{2,1,0:T(8,128)(2,1)} %inp_ref.1, bf16[2304,2048]{1,0:T(8,128)(2,1)} %bitcast.15, bf16[144,2048]{1,0:T(8,128)(2,1)} %bitcast.19, bf16[4,32,2304]{2,1,0:T(8,128)(2,1)} %cot_ref.1, s32[4]{0:T(128)} %len_ref.1), custom_call_target="tpu_custom_call" | custom-call | tf_op jit(solution)/shard_map/pallas_call | solution.py:321
  243.8 1.3 fusion
  245.1 1.2 fusion.1
  246.3 0.0 copy-start
  246.3 5.2 %convolution_convert_fusion.1 = bf16[128,2048]{1,0:T(8,128)(2,1)S(1)} fusion(bf16[128,2304]{1,0:T(8,128)(2,1)S(1)} %bitcast.17, bf16[1,2304,2048]{2,1,0:T(8,128)(2,1)} %param.6), kind=kOutput, calls=%fused_computation.1 | convolution fusion | flops 1208221696 | bytes 10551296 | tf_op jit(solution)/shard_map/dot_general | solution.py:19
  251.6 0.3 fusion.4
  251.8 0.0 copy-done
  251.8 0.4 fusion.2
  252.2 28.7 %psum.7 = f32[4]{0:T(128)S(1)} all-reduce(f32[4]{0:T(128)S(1)} %fusion.2), channel_id=1, replica_groups=mesh['section'=16,'dp'=16] {'section'}, use_global_device_ids=true, to_apply=%region_2.0 | all-reduce | flops 4 | bytes 32 | tf_op jit(solution)/shard_map/psum | solution.py:365
  281.0 0.2 multiply_convert_fusion
  281.2 5.1 %convolution_convert_fusion = bf16[2304,2048]{1,0:T(8,128)(2,1)} fusion(bf16[128,2304]{1,0:T(8,128)(2,1)S(1)} %bitcast.18, bf16[128,2048]{1,0:T(8,128)(2,1)S(1)} %convolution_convert_fusion.1), kind=kOutput, calls=%fused_computation | convolution fusion | flops 1212678144 | bytes 10551296 | tf_op jit(solution)/shard_map/dot_general | solution.py:27
  286.2 0.0 reduce-scatter.2.cloned.1.call-update
  286.2 62.5 %reduce-scatter.2.cloned.1.call-done = bf16[144,2048]{1,0:T(8,128)(2,1)} async-done(((bf16[2304,2048]{1,0:T(8,128)(2,1)}), bf16[144,2048]{1,0:T(8,128)(2,1)}) %reduce-scatter.2.cloned.1.call-update) | async-done | bytes 589840 | tf_op jit(solution)/shard_map/reduce_scatter | solution.py:368
  (2 shorter events, 0.0 us)
Async XLA Ops:
  6.5 342.2 %reduce-scatter.2.cloned.1.call-start = ((), (), s32[]{:S(2)}) async-start(), calls=%async_computation.1 | async-start | bytes 10027008 | tf_op jit(solution)/shard_map/reduce_scatter | solution.py:368
  246.3 5.5 %copy-start = (bf16[4,32,2304]{2,1,0:T(8,128)(2,1)S(1)}, bf16[4,32,2304]{2,1,0:T(8,128)(2,1)}, u32[]{:S(2)}) copy-start(bf16[4,32,2304]{2,1,0:T(8,128)(2,1)} %get-tuple-element.7) | copy-start | bytes 1769476
Sparse Core Ops, SparseCore 0:
  286.4 62.3 reduce-scatter.1

commit v2 on v1

--- a/solution.py
+++ b/solution.py
@@ -23,10 +23,6 @@
     return lax.dot_general(a, b, (((1,), (1,)), ((), ())), preferred_element_type=F32)
 
 
-def dot_tn(a, b):
-    return lax.dot_general(a, b, (((0,), (0,)), ((), ())), preferred_element_type=F32)
-
-
 def pick(cond, fn):
     def run():
         fn()
@@ -35,12 +31,15 @@
 
 
 def relay_kernel(
-    cfg, inp_ref, value_ref, slice_ref, cot_ref, len_ref, hk_ref, gk_ref,
+    cfg, inp_ref, value_ref, slice_ref, cot_ref, len_ref, out_ref,
     vbuf, wbuf, pbuf, tbuf, hbuf, obuf, gbuf, qbuf, ubuf,
+    grams, cols, turned, staged, parts, scales,
     load_sem, sib_sem, ring_send, ring_recv, h_send, h_recv, g_send, g_recv,
-    keep_send, keep_recv,
+    keep_send, keep_recv, col_send, col_recv, part_send, part_recv, scale_send, scale_recv, out_sem,
 ):
-    secs, chips, per, width, cw, nch, tsec = cfg
+    secs, chips, per, width, cw, nch, tsec, clip_scale = cfg
+    seq, features = hbuf.shape[1], vbuf.shape[1]
+    span, own_cols = cols.shape[2], width // chips
     half_ring = chips // 2
     rows_sl = slice_ref.shape[0]
     count = 2 * per
@@ -57,9 +56,30 @@
     first, last = sec == 0, sec == secs - 1
 
     barrier = pltpu.get_barrier_semaphore()
-    for dev in (sib, up, down, nxt, prv):
+
+    def greet(dev):
         pl.semaphore_signal(barrier, inc=1, device_id=dev, device_id_type=MESH)
-    pl.semaphore_wait(barrier, 5)
+
+    def others(total, me, fn):
+        def one(i, _):
+            fn(lax.rem(me + i, total))
+            return 0
+
+        lax.fori_loop(1, total, one, 0)
+
+    def greet_relay():
+        for dev in (up, down, nxt, prv):
+            greet(dev)
+        pl.semaphore_wait(barrier, 5)
+
+    def greet_helper():
+        others(chips, chip, lambda i: greet((sec, 2 * i)))
+        others(secs, sec, lambda i: greet((i, dp)))
+        pl.semaphore_wait(barrier, chips + secs - 1)
+
+    greet(sib)
+    pick(core == 1, greet_relay)
+    pick(core == 0, greet_helper)
 
     def remote(src, dst, send, recv, dev):
         return pltpu.make_async_remote_copy(
@@ -70,23 +90,20 @@
         return wbuf.at[pl.ds(pl.multiple_of(index * rows_sl, 16), rows_sl), :]
 
     def mask_rows(slot, position):
-        seq = gbuf.shape[1]
         live = lax.broadcasted_iota(jnp.int32, (seq, 1), 0) < len_ref[position]
         gbuf[slot] = jnp.where(live, gbuf[slot].astype(F32), 0.0).astype(BF16)
 
-    def keep(src, dst_ref, kind, mb):
-        def far():
-            remote(src, dst_ref.at[mb], keep_send.at[kind, mb], keep_recv.at[kind, mb], sib).start()
-
-        def near():
-            pltpu.make_async_copy(src, dst_ref.at[mb - per], keep_send.at[kind, mb]).start()
-
-        pick(mb < per, far)
-        pick(mb >= per, near)
+    def keep(src, dst, kind, mb):
+        return remote(src.at[mb], dst.at[mb], keep_send.at[kind, mb], keep_recv.at[kind, mb], sib)
+
+    def inv_rms(h32):
+        return lax.rsqrt(jnp.mean(h32 * h32, axis=-1, keepdims=True) + EPS)
 
     def helper_core():
         to_sib = remote(slice_ref, slice_rows(2 * chip), sib_sem.at[0], sib_sem.at[1], sib)
         to_sib.start()
+        load_v = pltpu.make_async_copy(value_ref, vbuf, load_sem.at[per])
+        load_v.start()
 
         def send_inputs():
             for i in range(per):
@@ -107,9 +124,151 @@
         pick(first, send_inputs)
         pick(last, send_cot)
         to_sib.wait_send()
-        for i in range(per):
-            remote(hbuf.at[i], hk_ref.at[i], keep_send.at[0, i], keep_recv.at[0, i], sib).wait_recv()
-            remote(gbuf.at[i], gk_ref.at[i], keep_send.at[1, i], keep_recv.at[1, i], sib).wait_recv()
+        load_v.wait()
+        block_rows = count * seq // 2
+        act = pbuf.at[:, pl.ds(0, features)]
+
+        def act_rows(index, rows=block_rows):
+            return act.at[pl.ds(pl.multiple_of(index * rows, 16), rows), :]
+
+        def make_values(mb, _):
+            keep(hbuf, obuf, 0, mb).wait_recv()
+            h32 = obuf[mb].astype(F32)
+            normed = (h32 * inv_rms(h32)).astype(BF16)
+            row = pl.multiple_of(chip * count * seq + mb * seq, 16)
+            gram = jnp.zeros((seq, seq), F32)
+            for c in range(2):
+                cols_c = slice(c * features // 2, (c + 1) * features // 2)
+                part = dot_nn(normed, vbuf[:, cols_c]).astype(BF16)
+                pbuf[pl.ds(row, seq), cols_c] = part
+                gram = gram + dot_nt(part, part)
+            grams[mb] = gram
+            return 0
+
+        lax.fori_loop(0, count, make_values, 0)
+
+        def ring(way, dist, half):
+            step = dist - 1
+            origin = lax.rem(chip + chips - step, chips) if way == 0 else lax.rem(chip + step, chips)
+            block = act_rows(2 * origin + half)
+            dev = up if way == 0 else down
+            return remote(block, block, ring_send.at[way, step, half], ring_recv.at[way, step, half], dev)
+
+        def arrived(way, dist, half):
+            origin = lax.rem(chip + chips - dist, chips) if way == 0 else lax.rem(chip + dist, chips)
+            block = act_rows(2 * origin + half)
+            remote(
+                block, block, ring_send.at[way, dist - 1, half], ring_recv.at[way, dist - 1, half], up
+            ).wait_recv()
+
+        for half in (1, 0):
+            for way in range(2):
+                ring(way, 1, half).start()
+
+        def ring_event(e, _):
+            dist, half = lax.div(e + 1, 2), lax.rem(e, 2)
+            arrived(0, dist, half)
+            pick(jnp.logical_or(dist + 1 < half_ring, half == 0), ring(0, dist + 1, half).start)
+            arrived(1, dist, half)
+            pick(jnp.logical_or(dist + 1 < half_ring, half == 1), ring(1, dist + 1, half).start)
+            return 0
+
+        lax.fori_loop(1, 2 * half_ring - 1, ring_event, 0)
+        arrived(0, half_ring, 0)
+        arrived(1, half_ring, 1)
+
+        def col_start(owner):
+            start = jnp.minimum(lax.div(owner * own_cols, 128) * 128, width - span)
+            return pl.multiple_of(start, 128)
+
+        def col_rows(mb):
+            return pl.ds(pl.multiple_of(mb * seq, 16), seq)
+
+        def make_parts(mb, _):
+            keep(gbuf, qbuf, 1, mb).wait_recv()
+
+            def to_owner(owner):
+                remote(
+                    qbuf.at[mb, :, pl.ds(col_start(owner), span)], cols.at[chip, col_rows(mb), :],
+                    col_send.at[owner], col_recv.at[chip], (sec, 2 * owner),
+                ).start()
+
+            others(chips, chip, to_owner)
+            cols[chip, col_rows(mb), :] = qbuf[mb, :, pl.ds(col_start(chip), span)]
+            g = qbuf[mb]
+            part = jnp.sum(grams[mb] * dot_nt(g, g), keepdims=True)
+            parts[sec, pl.ds(mb, 1), :] = jnp.broadcast_to(part, (1, 128))
+            return 0
+
+        lax.fori_loop(0, count, make_parts, 0)
+
+        def part_copy(to, slot):
+            return remote(parts.at[slot], parts.at[slot], part_send.at[to], part_recv.at[slot], (to, dp))
+
+        def scale_copy(to, slot):
+            return remote(
+                scales.at[slot], scales.at[slot], scale_send.at[to], scale_recv.at[slot], (sec, 2 * to)
+            )
+
+        others(secs, sec, lambda to: part_copy(to, sec).start())
+        block = count * seq
+
+        def col_copy(owner, source):
+            return remote(cols.at[source], cols.at[source], col_send.at[owner], col_recv.at[source], sib)
+
+        def turn(i, _):
+            source = lax.rem(chip + i, chips)
+            pick(i > 0, col_copy(source, source).wait_recv)
+            turned[:, pl.ds(pl.multiple_of(source * block, 128), block)] = cols[source].T
+            return 0
+
+        lax.fori_loop(0, chips, turn, 0)
+        others(secs, sec, lambda i: part_copy(i, i).wait_recv())
+        totals = jnp.sum(parts[...], axis=0)
+        scales[chip] = clip_scale / (jnp.sqrt(totals) + GAMMA)
+        others(chips, chip, lambda to: scale_copy(to, chip).start())
+        others(chips, chip, lambda i: scale_copy(i, i).wait_recv())
+        lane = lax.broadcasted_iota(jnp.int32, (1, 128), 1)
+        group = 128 // seq
+        for tile in range(chips * block // 128):
+            row = jnp.zeros((1, 128), F32)
+            for k in range(group):
+                example = tile * group + k
+                value = scales[example // count, example % count:example % count + 1, :]
+                row = jnp.where(lax.div(lane, seq) == k, value, row)
+            at = slice(tile * 128, (tile + 1) * 128)
+            turned[:, at] = (turned[:, at].astype(F32) * row).astype(BF16)
+
+        rows_own = pl.ds(pl.multiple_of(chip * own_cols - col_start(chip), 16), own_cols)
+        nout = 4
+        cf = features // nout
+
+        def out_copies(c):
+            piece = pl.ds(c * cf, cf)
+            near = pltpu.make_async_copy(staged.at[pl.ds(0, rows_sl), piece], out_ref.at[:, piece], out_sem.at[c])
+            far = remote(
+                staged.at[pl.ds(rows_sl, rows_sl), piece], out_ref.at[:, piece],
+                out_sem.at[nout + c], out_sem.at[2 * nout], sib,
+            )
+            return near, far
+
+        for c in range(nout):
+            at = slice(c * cf, (c + 1) * cf)
+            staged[:, at] = dot_nn(turned[rows_own, :], pbuf[:chips * block, at]).astype(BF16)
+            for copy in out_copies(c):
+                copy.start()
+        for c in range(nout):
+            near, far = out_copies(c)
+            near.wait()
+            far.wait_send()
+        others(secs, sec, lambda to: part_copy(to, sec).wait_send())
+        others(chips, chip, lambda to: scale_copy(to, chip).wait_send())
+        others(chips, chip, lambda to: col_copy(to, chip).wait_send())
+        for way in range(2):
+            for dist in range(1, half_ring + 1):
+                for half in range(2):
+                    if dist < half_ring or half == way:
+                        ring(way, dist, half).wait_send()
 
     def relay_core():
         load_v = pltpu.make_async_copy(value_ref, vbuf, load_sem.at[0])
@@ -215,18 +374,15 @@
         def whole(buf, mb, send, recv, dev):
             return remote(buf.at[mb], buf.at[mb], send.at[mb], recv.at[mb], dev)
 
-        def inv_rms(h32):
-            return lax.rsqrt(jnp.mean(h32 * h32, axis=-1, keepdims=True) + EPS)
-
         def forward(mb, _):
             pick(jnp.logical_or(sec > 0, mb < per), whole(hbuf, mb, h_send, h_recv, sib).wait_recv)
-            keep(hbuf.at[mb], hk_ref, 0, mb)
+            keep(hbuf, obuf, 0, mb).start()
             h = hbuf[mb]
             h32 = h.astype(F32)
             r = inv_rms(h32)
             for c in range(nch):
                 cols = pl.ds(c * cn, cn)
-                u = dot_nn(h, pbuf[:, c * cn:(c + 1) * cn])
+                u = dot_nn(h, pbuf[:width, c * cn:(c + 1) * cn])
                 ubuf[mb, :, c * cn:(c + 1) * cn] = u
                 obuf[mb, :, c * cn:(c + 1) * cn] = (h32[:, c * cn:(c + 1) * cn] + r * u).astype(BF16)
                 remote(
@@ -245,7 +401,7 @@
 
         def backward(mb, _):
             whole(gbuf, mb, g_send, g_recv, sib).wait_recv()
-            keep(gbuf.at[mb], gk_ref, 1, mb)
+            keep(gbuf, qbuf, 1, mb).start()
             g = gbuf[mb]
             g32, h32 = g.astype(F32), hbuf[mb].astype(F32)
             r = inv_rms(h32)
@@ -259,9 +415,9 @@
 
         def backward_last(mb, _):
             pick(mb < per, whole(gbuf, mb, g_send, g_recv, sib).wait_recv)
-            keep(gbuf.at[mb], gk_ref, 1, mb)
+            keep(gbuf, qbuf, 1, mb).start()
             whole(hbuf, mb, h_send, h_recv, sib).wait_recv()
-            keep(hbuf.at[mb], hk_ref, 0, mb)
+            keep(hbuf, obuf, 0, mb).start()
             g = gbuf[mb]
             g32, h32 = g.astype(F32), hbuf[mb].astype(F32)
             r = inv_rms(h32)
@@ -281,7 +437,7 @@
 
         def backward_first(mb, _):
             whole(gbuf, mb, g_send, g_recv, sib).wait_recv()
-            keep(gbuf.at[mb], gk_ref, 1, mb)
+            keep(gbuf, qbuf, 1, mb).start()
             return 0
 
         pick(last, lambda: lax.fori_loop(0, count, backward_last, 0))
@@ -294,9 +450,8 @@
         def drain(mb, _):
             pick(sec < secs - 1, whole(hbuf, mb, h_send, h_recv, nxt).wait_send)
             pick(sec > 0, whole(gbuf, mb, g_send, g_recv, prv).wait_send)
-            for kind, buf, out in ((0, hbuf, hk_ref), (1, gbuf, gk_ref)):
-                pick(mb < per, remote(buf.at[mb], out.at[0], keep_send.at[kind, mb], keep_recv.at[kind, mb], sib).wait_send)
-                pick(mb >= per, pltpu.make_async_copy(buf.at[mb], out.at[0], keep_send.at[kind, mb]).wait)
+            keep(hbuf, obuf, 0, mb).wait_send()
+            keep(gbuf, qbuf, 1, mb).wait_send()
             return 0
 
         lax.fori_loop(0, count, drain, 0)
@@ -305,34 +460,45 @@
                 for half in range(2):
                     if dist < half_ring or half == way:
                         ring(way, dist, half).wait_send()
+        remote(out_ref, out_ref, out_sem.at[0], out_sem.at[out_sem.shape[0] - 1], sib).wait_recv()
 
     pick(core == 0, helper_core)
     pick(core == 1, relay_core)
 
 
-def relay(inputs, value_weight, output_weight, cotangent, lengths, cw, nch, tsec):
+def per_device(inputs, value_weight, output_weight, cotangent, lengths, cw=256, nch=3, tsec=10):
     per, seq, width = inputs.shape
-    features = value_weight.shape[1]
+    features = value_weight.shape[2]
+    rows_sl = output_weight.shape[1]
     secs, chips = lax.axis_size("section"), lax.axis_size("dp") // 2
     count = 2 * per
+    own = width // chips
+    span = max(-(-(i * own + own) // 128) - (i * own) // 128 for i in range(chips)) * 128
+    clip_scale = math.sqrt(features * width * 1.0 / (count * chips))
     any_spec = pl.BlockSpec(memory_space=pl.ANY)
-    keep = jax.ShapeDtypeStruct((per, seq, width), BF16)
     dma = pltpu.SemaphoreType.DMA
-    return pl.pallas_call(
-        functools.partial(relay_kernel, (secs, chips, per, width, cw, nch, tsec)),
-        out_shape=(keep, keep),
+    tall, wide = max(width, chips * count * seq), max(width, features)
+    result = pl.pallas_call(
+        functools.partial(relay_kernel, (secs, chips, per, width, cw, nch, tsec, clip_scale)),
+        out_shape=jax.ShapeDtypeStruct((rows_sl, features), BF16),
         in_specs=[any_spec] * 4 + [pl.BlockSpec(memory_space=pltpu.SMEM)],
-        out_specs=(any_spec, any_spec),
+        out_specs=any_spec,
         scratch_shapes=[
             pltpu.VMEM((width, features), BF16),
             pltpu.VMEM((width, features), BF16),
-            pltpu.VMEM((width, width), BF16),
+            pltpu.VMEM((tall, wide), BF16),
             pltpu.VMEM((width, width), BF16),
             pltpu.VMEM((count, seq, width), BF16),
             pltpu.VMEM((count, seq, width), BF16),
             pltpu.VMEM((count, seq, width), BF16),
             pltpu.VMEM((count, seq, width), BF16),
             pltpu.VMEM((count, seq, width), F32),
+            pltpu.VMEM((count, seq, seq), F32),
+            pltpu.VMEM((chips, count * seq, span), BF16),
+            pltpu.VMEM((span, chips * count * seq), BF16),
+            pltpu.VMEM((own, features), BF16),
+            pltpu.VMEM((secs, count, 128), F32),
+            pltpu.VMEM((chips, count, 128), F32),
             dma((per + 4,)),
             dma((2,)),
             dma((2, chips // 2, 2)),
@@ -343,32 +509,19 @@
             dma((count,)),
             dma((2, count)),
             dma((2, count)),
+            dma((chips,)),
+            dma((chips,)),
+            dma((secs,)),
+            dma((secs,)),
+            dma((chips,)),
+            dma((chips,)),
+            dma((9,)),
         ],
         compiler_params=pltpu.CompilerParams(
             collective_id=0, has_side_effects=True, vmem_limit_bytes=60 << 20
         ),
-    )(inputs, value_weight, output_weight, cotangent, lengths)
-
-
-def per_device(inputs, value_weight, output_weight, cotangent, lengths, cw=256, nch=3, tsec=10):
-    per, seq, width = inputs.shape
-    w_value = value_weight[0]
-    features = w_value.shape[1]
-    clip_scale = math.sqrt(features * width * 1.0 / (per * lax.axis_size("dp")))
-    hidden, grads = relay(inputs, w_value, output_weight[0], cotangent, lengths, cw, nch, tsec)
-    h32 = hidden.astype(F32)
-    normed = (h32 * lax.rsqrt(jnp.mean(h32 * h32, axis=-1, keepdims=True) + EPS)).astype(BF16)
-    values = dot_nn(normed.reshape(per * seq, width), w_value).astype(BF16)
-    v3 = values.reshape(per, seq, features)
-    gram_v = jnp.einsum("etf,esf->ets", v3, v3, preferred_element_type=F32)
-    gram_g = jnp.einsum("etc,esc->ets", grads, grads, preferred_element_type=F32)
-    totals = lax.psum(jnp.sum(gram_v * gram_g, axis=(1, 2)), "section")
-    factors = clip_scale / (jnp.sqrt(totals) + GAMMA)
-    weighted = (grads.astype(F32) * factors[:, None, None]).astype(BF16)
-    summed = lax.psum_scatter(
-        dot_tn(weighted.reshape(per * seq, width), values).astype(BF16), "dp", scatter_dimension=0, tiled=True
-    )
-    return summed[None]
+    )(inputs, value_weight[0], output_weight[0], cotangent, lengths)
+    return result[None]
 
 
 def solution(mesh):

time: 358 us -> 262 us (0.73)
  waiting for transfers between devices: 62.5 us -> 0 us
  blocking collectives: 28.7 us -> 0 us
  Pallas kernels: 237 us -> 260 us
  between operations: 13.4 us -> 0.01 us
  matrix products: 10.9 us -> 0 us
    reduce_scatter x1 -> x0, waiting for transfers between devices: 62.5 us -> none  [per_device(): lax.psum_scatter(dot_tn(weighted.reshape(per * seq, width), values).astyp...]
    psum x1 -> x0, blocking collectives: 28.7 us -> none  [per_device(): totals = lax.psum(jnp.sum(gram_v * gram_g, axis=(1, 2)), 'section')]
    pallas_call x1, Pallas kernels: 237 us -> 260 us  [per_device(): pl.pallas_call(functools.partial(relay_kernel, (secs, chips, per, width,...]
    dot_general x4 -> x0, matrix products: 10.9 us -> none  [the longest x1 5.21 us: dot_nn(): lax.dot_general(a, b, (((1,), (0,)), ((), ())), preferred_element_type=F32)]
  transfers between devices with their start and end apart: 1 -> 0, of which waited for: 1 -> 0; matrix products, arithmetic and copies ran while one was open for 0% -> 0% of each run, Pallas kernels for 0% -> 0%
where the time goes in v2:
time: 262 us
  Pallas kernels  260 us (99%)
    pallas_call x1, Pallas kernels, per_device(): pl.pallas_call(functools.partial(relay_kernel, (secs, chips, per, width,...  260 us

profile of v2, /device:TPU:1, one launch (start us, length us, event | category | flops | bytes accessed | tf_op | source)
XLA Modules:
  0.0 261.5 jit_solution(15003760347951102161)
XLA Ops:
  0.0 259.6 %shard_map.55 = bf16[144,2048]{1,0:T(8,128)(2,1)} custom-call(bf16[4,32,2304]{2,1,0:T(8,128)(2,1)} %inp_ref.1, bf16[2304,2048]{1,0:T(8,128)(2,1)} %bitcast.3, bf16[144,2048]{1,0:T(8,128)(2,1)} %bitcast.5, bf16[4,32,2304]{2,1,0:T(8,128)(2,1)} %cot_ref.1, s32[4]{0:T(128)} %len_ref.1), custom_call_target="tpu_custom_call" | custom-call | tf_op jit(solution)/shard_map/pallas_call | solution.py:481
  259.6 1.9 copy.7

commit v3 on v2

--- a/solution.py
+++ b/solution.py
@@ -11,6 +11,7 @@
 EPS = 1e-06
 GAMMA = 0.01
 MESH = pl.DeviceIdType.MESH
+CUTS = (0, 1280, 2304)
 F32 = jnp.float32
 BF16 = jnp.bfloat16
 
@@ -21,6 +22,12 @@
 
 def dot_nt(a, b):
     return lax.dot_general(a, b, (((1,), (1,)), ((), ())), preferred_element_type=F32)
+
+
+def dot_tall(a, b):
+    rows = a.shape[0]
+    tall = jnp.concatenate([a] * (128 // rows), axis=0)
+    return dot_nn(tall, b)[:rows]
 
 
 def pick(cond, fn):
@@ -37,11 +44,13 @@
     load_sem, sib_sem, ring_send, ring_recv, h_send, h_recv, g_send, g_recv,
     keep_send, keep_recv, col_send, col_recv, part_send, part_recv, scale_send, scale_recv, out_sem,
 ):
-    secs, chips, per, width, cw, nch, tsec, clip_scale = cfg
+    secs, chips, per, width, cw, nch, tsec, cuts, clip_scale = cfg
     seq, features = hbuf.shape[1], vbuf.shape[1]
     span, own_cols = cols.shape[2], width // chips
     half_ring = chips // 2
     rows_sl = slice_ref.shape[0]
+    pieces = 3
+    rows_pc = rows_sl // pieces
     count = 2 * per
     cn = width // nch
     sec = lax.axis_index("section")
@@ -55,31 +64,38 @@
     prv = (lax.rem(sec + secs - 1, secs), dp)
     first, last = sec == 0, sec == secs - 1
 
+    part_rows = width // 4
+
+    def load_values(wait):
+        for i in range(4):
+            rows = pl.ds(i * part_rows, part_rows)
+            copy = pltpu.make_async_copy(value_ref.at[rows, :], vbuf.at[rows, :], load_sem.at[per + i])
+            copy.wait() if wait else copy.start()
+
+    load_values(wait=False)
     barrier = pltpu.get_barrier_semaphore()
 
     def greet(dev):
         pl.semaphore_signal(barrier, inc=1, device_id=dev, device_id_type=MESH)
 
     def others(total, me, fn):
-        def one(i, _):
-            fn(lax.rem(me + i, total))
-            return 0
-
-        lax.fori_loop(1, total, one, 0)
+        if total == 16:
+            far = (0, 1, 2, 1)
+            steps = sorted(range(1, 16), key=lambda i: -far[i // 4] - far[i % 4])
+            for i in steps:
+                row, col = lax.rem(lax.div(me, 4) + i // 4, 4), lax.rem(lax.rem(me, 4) + i % 4, 4)
+                fn(row * 4 + col)
+        else:
+            for i in sorted(range(1, total), key=lambda i: -min(i, total - i)):
+                fn(lax.rem(me + i, total))
 
     def greet_relay():
-        for dev in (up, down, nxt, prv):
+        for dev in (up, down, nxt, prv, sib):
             greet(dev)
-        pl.semaphore_wait(barrier, 5)
-
-    def greet_helper():
-        others(chips, chip, lambda i: greet((sec, 2 * i)))
-        others(secs, sec, lambda i: greet((i, dp)))
-        pl.semaphore_wait(barrier, chips + secs - 1)
-
-    greet(sib)
+        pl.semaphore_wait(barrier, 4)
+
     pick(core == 1, greet_relay)
-    pick(core == 0, greet_helper)
+    pick(core == 0, lambda: pl.semaphore_wait(barrier, 1))
 
     def remote(src, dst, send, recv, dev):
         return pltpu.make_async_remote_copy(
@@ -102,9 +118,6 @@
     def helper_core():
         to_sib = remote(slice_ref, slice_rows(2 * chip), sib_sem.at[0], sib_sem.at[1], sib)
         to_sib.start()
-        load_v = pltpu.make_async_copy(value_ref, vbuf, load_sem.at[per])
-        load_v.start()
-
         def send_inputs():
             for i in range(per):
                 remote(inp_ref.at[i], hbuf.at[i], h_send.at[i], h_recv.at[i], sib).start()
@@ -124,7 +137,7 @@
         pick(first, send_inputs)
         pick(last, send_cot)
         to_sib.wait_send()
-        load_v.wait()
+        load_values(wait=True)
         block_rows = count * seq // 2
         act = pbuf.at[:, pl.ds(0, features)]
 
@@ -161,9 +174,11 @@
                 block, block, ring_send.at[way, dist - 1, half], ring_recv.at[way, dist - 1, half], up
             ).wait_recv()
 
-        for half in (1, 0):
-            for way in range(2):
-                ring(way, 1, half).start()
+        for way in range(2):
+            ring(way, 1, 1).start()
+        for way in range(2):
+            ring(way, 1, 1).wait_send()
+            ring(way, 1, 0).start()
 
         def ring_event(e, _):
             dist, half = lax.div(e + 1, 2), lax.rem(e, 2)
@@ -267,41 +282,47 @@
         for way in range(2):
             for dist in range(1, half_ring + 1):
                 for half in range(2):
-                    if dist < half_ring or half == way:
+                    if (dist < half_ring or half == way) and (dist, half) != (1, 1):
                         ring(way, dist, half).wait_send()
 
     def relay_core():
-        load_v = pltpu.make_async_copy(value_ref, vbuf, load_sem.at[0])
-        load_w = pltpu.make_async_copy(slice_ref, slice_rows(2 * chip + 1), load_sem.at[1])
-        load_in = pltpu.make_async_copy(inp_ref, hbuf.at[pl.ds(per, per)], load_sem.at[2])
-        load_cot = pltpu.make_async_copy(cot_ref, gbuf.at[pl.ds(per, per)], load_sem.at[3])
-
-        def ring(way, dist, half, src=None):
+        load_w = pltpu.make_async_copy(slice_ref, slice_rows(2 * chip + 1), load_sem.at[0])
+        load_in = pltpu.make_async_copy(inp_ref, hbuf.at[pl.ds(per, per)], load_sem.at[1])
+        load_cot = pltpu.make_async_copy(cot_ref, gbuf.at[pl.ds(per, per)], load_sem.at[2])
+        load_w.start()
+        pick(first, load_in.start)
+        pick(last, load_cot.start)
+        turns = 2 * pieces
+
+        def piece_rows(origin, order):
+            index = origin * turns + lax.rem(order + pieces, turns)
+            return wbuf.at[pl.ds(pl.multiple_of(index * rows_pc, 16), rows_pc), :]
+
+        def ring(way, dist, order, src=None):
             step = dist - 1
             origin = lax.rem(chip + chips - step, chips) if way == 0 else lax.rem(chip + step, chips)
-            block = slice_rows(2 * origin + half)
+            block = piece_rows(origin, order)
             dev = up if way == 0 else down
             return remote(
                 block if src is None else src, block,
-                ring_send.at[way, step, half], ring_recv.at[way, step, half], dev,
+                ring_send.at[way, step, order], ring_recv.at[way, step, order], dev,
             )
 
-        def arrived(way, dist, half):
+        def arrived(way, dist, order):
             origin = lax.rem(chip + chips - dist, chips) if way == 0 else lax.rem(chip + dist, chips)
-            block = slice_rows(2 * origin + half)
+            block = piece_rows(origin, order)
             remote(
-                block, block, ring_send.at[way, dist - 1, half], ring_recv.at[way, dist - 1, half], up
+                block, block, ring_send.at[way, dist - 1, order], ring_recv.at[way, dist - 1, order], up
             ).wait_recv()
 
-        for way in range(2):
-            ring(way, 1, 1, slice_ref).start()
-        load_w.start()
-        load_v.start()
-        pick(first, load_in.start)
-        pick(last, load_cot.start)
-        remote(slice_ref, slice_rows(2 * chip), sib_sem.at[0], sib_sem.at[1], sib).wait_recv()
-        for way in range(2):
-            ring(way, 1, 0).start()
+        for order in range(turns):
+            if order == pieces:
+                remote(slice_ref, slice_rows(2 * chip), sib_sem.at[0], sib_sem.at[1], sib).wait_recv()
+            src = slice_ref.at[pl.ds(order * rows_pc, rows_pc), :] if order < pieces else None
+            for way in range(2):
+                if order >= pieces:
+                    ring(way, 1, order - pieces).wait_send()
+                ring(way, 1, order, src).start()
         pick(first, load_in.wait)
 
         def ready_cot():
@@ -311,22 +332,21 @@
 
         pick(last, ready_cot)
         load_w.wait()
-        load_v.wait()
-
-        def slice_event(index):
-            gap = lax.rem(lax.div(index, 2) + chips - chip, chips)
-            dist = jnp.minimum(gap, chips - gap)
-            near = 2 * dist - lax.rem(index, 2)
-            return jnp.where(dist == 0, 0, jnp.where(dist == half_ring, 2 * half_ring - 1, near))
-
-        def chunk_event(j):
-            lo, hi = lax.div(cw * j, rows_sl), lax.div(cw * j + cw - 1, rows_sl)
-            event = slice_event(lo)
-            for extra in range(1, cw // rows_sl + 2):
-                event = jnp.maximum(event, slice_event(jnp.minimum(lo + extra, hi)))
-            return event
-
-        def make_p(event):
+        load_values(wait=True)
+        chunks = width // cw
+
+        def chip_gap(index):
+            gap = lax.rem(index + chips - chip, chips)
+            return jnp.minimum(gap, chips - gap)
+
+        def chunk_level(j):
+            rows = 2 * rows_sl
+            level = chip_gap(lax.div(cw * j, rows))
+            for extra in range(1, (cw - 2) // rows + 2):
+                level = jnp.maximum(level, chip_gap(lax.div(jnp.minimum(cw * j + extra * rows, cw * j + cw - 1), rows)))
+            return level
+
+        def make_p(level, start, number):
             def chunk(j, _):
                 def run():
                     off = pl.multiple_of(j * cw, cw)
@@ -334,30 +354,32 @@
                         block = dot_nt(vbuf[m * cn:(m + 1) * cn, :], wbuf[pl.ds(off, cw), :])
                         pbuf[m * cn:(m + 1) * cn, pl.ds(off, cw)] = block.astype(BF16)
 
-                pick(chunk_event(j) == event, run)
+                pick(jnp.logical_and(j < chunks, chunk_level(jnp.minimum(j, chunks - 1)) == level), run)
                 return 0
 
-            lax.fori_loop(0, width // cw, chunk, 0)
+            lax.fori_loop(start, start + number, chunk, 0)
 
         def ring_event(e, _):
-            dist, half = lax.div(e + 1, 2), lax.rem(e, 2)
-
-            def turn():
-                arrived(0, dist, half)
-                pick(jnp.logical_or(dist + 1 < half_ring, half == 0), ring(0, dist + 1, half).start)
-                arrived(1, dist, half)
-                pick(jnp.logical_or(dist + 1 < half_ring, half == 1), ring(1, dist + 1, half).start)
-
-            def final():
-                arrived(0, half_ring, 0)
-                arrived(1, half_ring, 1)
-
-            pick(jnp.logical_and(e > 0, e < 2 * half_ring - 1), turn)
-            pick(e == 2 * half_ring - 1, final)
-            make_p(e)
-            return 0
-
-        lax.fori_loop(0, 2 * half_ring, ring_event, 0)
+            dist, order = lax.div(e, turns) + 1, lax.rem(e, turns)
+            arrived(0, dist, order)
+            pick(jnp.logical_or(dist + 1 < half_ring, order < pieces), ring(0, dist + 1, order).start)
+            arrived(1, dist, order)
+            pick(jnp.logical_or(dist + 1 < half_ring, order >= pieces), ring(1, dist + 1, order).start)
+            each = -(-chunks // turns)
+            make_p(dist - 1, order * each, each)
+            return 0
+
+        lax.fori_loop(0, (half_ring - 1) * turns, ring_event, 0)
+
+        def final_event(k, _):
+            arrived(0, half_ring, k)
+            arrived(1, half_ring, k + pieces)
+            each = -(-chunks // pieces)
+            make_p(half_ring - 1, k * each, each)
+            return 0
+
+        lax.fori_loop(0, pieces, final_event, 0)
+        make_p(half_ring, 0, chunks)
 
         def make_t():
             def chunk(j, _):
@@ -376,41 +398,46 @@
 
         def forward(mb, _):
             pick(jnp.logical_or(sec > 0, mb < per), whole(hbuf, mb, h_send, h_recv, sib).wait_recv)
-            keep(hbuf, obuf, 0, mb).start()
             h = hbuf[mb]
             h32 = h.astype(F32)
             r = inv_rms(h32)
-            for c in range(nch):
-                cols = pl.ds(c * cn, cn)
-                u = dot_nn(h, pbuf[:width, c * cn:(c + 1) * cn])
-                ubuf[mb, :, c * cn:(c + 1) * cn] = u
-                obuf[mb, :, c * cn:(c + 1) * cn] = (h32[:, c * cn:(c + 1) * cn] + r * u).astype(BF16)
+            for lo, hi in zip(cuts, cuts[1:]):
+                piece = pl.ds(lo, hi - lo)
+                u = dot_tall(h, pbuf[:width, lo:hi])
+                ubuf[mb, :, lo:hi] = u
+                obuf[mb, :, lo:hi] = (h32[:, lo:hi] + r * u).astype(BF16)
                 remote(
-                    obuf.at[mb, :, cols], hbuf.at[mb, :, cols], h_send.at[mb], h_recv.at[mb], nxt
+                    obuf.at[mb, :, piece], hbuf.at[mb, :, piece], h_send.at[mb], h_recv.at[mb], nxt
                 ).start()
+            keep(hbuf, obuf, 0, mb).start()
             return 0
 
         pick(sec < secs - 1, lambda: lax.fori_loop(0, count, forward, 0))
         pick(jnp.logical_and(sec > 0, sec < tsec), make_t)
 
-        def send_grad(mb, c):
-            cols = pl.ds(c * cn, cn)
+        def send_grad(mb, lo, hi):
+            piece = pl.ds(lo, hi - lo)
             remote(
-                qbuf.at[mb, :, cols], gbuf.at[mb, :, cols], g_send.at[mb], g_recv.at[mb], prv
+                qbuf.at[mb, :, piece], gbuf.at[mb, :, piece], g_send.at[mb], g_recv.at[mb], prv
             ).start()
 
-        def backward(mb, _):
-            whole(gbuf, mb, g_send, g_recv, sib).wait_recv()
-            keep(gbuf, qbuf, 1, mb).start()
-            g = gbuf[mb]
-            g32, h32 = g.astype(F32), hbuf[mb].astype(F32)
+        def backward(batch, step, _):
+            at = pl.ds(step * batch, batch)
+            for i in range(batch):
+                whole(gbuf, step * batch + i, g_send, g_recv, sib).wait_recv()
+            rows = batch * seq
+            g = gbuf[at].reshape(rows, width)
+            g32, h32 = g.astype(F32), hbuf[at].reshape(rows, width).astype(F32)
             r = inv_rms(h32)
-            coef = jnp.sum(g32 * ubuf[mb], axis=-1, keepdims=True) * (r * r * r) * (1.0 / width)
-            for c in range(nch):
-                lo, hi = c * cn, (c + 1) * cn
-                p = dot_nn(g, tbuf[:, lo:hi])
-                qbuf[mb, :, lo:hi] = (g32[:, lo:hi] + r * p - coef * h32[:, lo:hi]).astype(BF16)
-                send_grad(mb, c)
+            coef = jnp.sum(g32 * ubuf[at].reshape(rows, width), axis=-1, keepdims=True) * (r * r * r) * (1.0 / width)
+            for lo, hi in zip(cuts, cuts[1:]):
+                p = dot_tall(g, tbuf[:, lo:hi])
+                result = (g32[:, lo:hi] + r * p - coef * h32[:, lo:hi]).astype(BF16)
+                qbuf[at, :, lo:hi] = result.reshape(batch, seq, hi - lo)
+                for i in range(batch):
+                    send_grad(step * batch + i, lo, hi)
+            for i in range(batch):
+                keep(gbuf, qbuf, 1, step * batch + i).start()
             return 0
 
         def backward_last(mb, _):
@@ -422,17 +449,15 @@
             g32, h32 = g.astype(F32), hbuf[mb].astype(F32)
             r = inv_rms(h32)
             dots = jnp.zeros_like(r)
-            for c in range(nch):
-                lo, hi = c * cn, (c + 1) * cn
-                p = dot_nn(g, tbuf[:, lo:hi])
+            for lo, hi in zip(cuts, cuts[1:]):
+                p = dot_tall(g, tbuf[:, lo:hi])
                 ubuf[mb, :, lo:hi] = p
                 dots = dots + jnp.sum(p * h32[:, lo:hi], axis=-1, keepdims=True)
             coef = dots * (r * r * r) * (1.0 / width)
-            for c in range(nch):
-                lo, hi = c * cn, (c + 1) * cn
+            for lo, hi in zip(cuts, cuts[1:]):
                 p = ubuf[mb, :, lo:hi]
                 qbuf[mb, :, lo:hi] = (g32[:, lo:hi] + r * p - coef * h32[:, lo:hi]).astype(BF16)
-                send_grad(mb, c)
+                send_grad(mb, lo, hi)
             return 0
 
         def backward_first(mb, _):
@@ -442,8 +467,12 @@
 
         pick(last, lambda: lax.fori_loop(0, count, backward_last, 0))
         pick(
-            jnp.logical_and(sec > 0, sec < secs - 1),
-            lambda: lax.fori_loop(0, count, backward, 0),
+            jnp.logical_and(sec > 0, sec < secs - 2),
+            lambda: lax.fori_loop(0, count, functools.partial(backward, 1), 0),
+        )
+        pick(
+            jnp.logical_and(sec > 0, sec == secs - 2),
+            lambda: lax.fori_loop(0, count // 2, functools.partial(backward, 2), 0),
         )
         pick(first, lambda: lax.fori_loop(0, count, backward_first, 0))
 
@@ -457,16 +486,18 @@
         lax.fori_loop(0, count, drain, 0)
         for way in range(2):
             for dist in range(1, half_ring + 1):
-                for half in range(2):
-                    if dist < half_ring or half == way:
-                        ring(way, dist, half).wait_send()
+                for order in range(turns):
+                    if dist == half_ring and (order < pieces) != (way == 0):
+                        continue
+                    if dist > 1 or order >= pieces:
+                        ring(way, dist, order).wait_send()
         remote(out_ref, out_ref, out_sem.at[0], out_sem.at[out_sem.shape[0] - 1], sib).wait_recv()
 
     pick(core == 0, helper_core)
     pick(core == 1, relay_core)
 
 
-def per_device(inputs, value_weight, output_weight, cotangent, lengths, cw=256, nch=3, tsec=10):
+def per_device(inputs, value_weight, output_weight, cotangent, lengths, cw=256, nch=3, tsec=10, cuts=CUTS):
     per, seq, width = inputs.shape
     features = value_weight.shape[2]
     rows_sl = output_weight.shape[1]
@@ -479,7 +510,7 @@
     dma = pltpu.SemaphoreType.DMA
     tall, wide = max(width, chips * count * seq), max(width, features)
     result = pl.pallas_call(
-        functools.partial(relay_kernel, (secs, chips, per, width, cw, nch, tsec, clip_scale)),
+        functools.partial(relay_kernel, (secs, chips, per, width, cw, nch, tsec, cuts, clip_scale)),
         out_shape=jax.ShapeDtypeStruct((rows_sl, features), BF16),
         in_specs=[any_spec] * 4 + [pl.BlockSpec(memory_space=pltpu.SMEM)],
         out_specs=any_spec,
@@ -499,10 +530,10 @@
             pltpu.VMEM((own, features), BF16),
             pltpu.VMEM((secs, count, 128), F32),
             pltpu.VMEM((chips, count, 128), F32),
-            dma((per + 4,)),
+            dma((per + 7,)),
             dma((2,)),
-            dma((2, chips // 2, 2)),
-            dma((2, chips // 2, 2)),
+            dma((2, chips // 2, 6)),
+            dma((2, chips // 2, 6)),
             dma((count,)),
             dma((count,)),
             dma((count,)),

time: 262 us -> 244 us (0.931)
  Pallas kernels: 260 us -> 241 us
    pallas_call x1, Pallas kernels: 260 us -> 241 us  [per_device(): pl.pallas_call(functools.partial(relay_kernel, (secs, chips, per, width,...]
where the time goes in v3:
time: 244 us; the launch traced here: 243 us
  Pallas kernels  241 us (99%)
    pallas_call x1, Pallas kernels, per_device(): pl.pallas_call(functools.partial(relay_kernel, (secs, chips, per, width,...  241 us

profile of v3, /device:TPU:1, one launch (start us, length us, event | category | flops | bytes accessed | tf_op | source)
XLA Modules:
  0.0 243.4 jit_solution(5420919778622988378)
XLA Ops:
  0.0 241.4 %shard_map.55 = bf16[144,2048]{1,0:T(8,128)(2,1)} custom-call(bf16[4,32,2304]{2,1,0:T(8,128)(2,1)} %inp_ref.1, bf16[2304,2048]{1,0:T(8,128)(2,1)} %bitcast.3, bf16[144,2048]{1,0:T(8,128)(2,1)} %bitcast.5, bf16[4,32,2304]{2,1,0:T(8,128)(2,1)} %cot_ref.1, s32[4]{0:T(128)} %len_ref.1), custom_call_target="tpu_custom_call" | custom-call | tf_op jit(solution)/shard_map/pallas_call | solution.py:512
  241.5 1.9 copy.7

commit v4 on v3

--- a/solution.py
+++ b/solution.py
@@ -208,11 +208,11 @@
                     col_send.at[owner], col_recv.at[chip], (sec, 2 * owner),
                 ).start()
 
-            others(chips, chip, to_owner)
-            cols[chip, col_rows(mb), :] = qbuf[mb, :, pl.ds(col_start(chip), span)]
             g = qbuf[mb]
             part = jnp.sum(grams[mb] * dot_nt(g, g), keepdims=True)
             parts[sec, pl.ds(mb, 1), :] = jnp.broadcast_to(part, (1, 128))
+            others(chips, chip, to_owner)
+            cols[chip, col_rows(mb), :] = qbuf[mb, :, pl.ds(col_start(chip), span)]
             return 0
 
         lax.fori_loop(0, count, make_parts, 0)
@@ -333,6 +333,16 @@
         pick(last, ready_cot)
         load_w.wait()
         load_values(wait=True)
+
+        def first_values():
+            for i in range(per):
+                remote(hbuf.at[i], hbuf.at[i], h_send.at[i], h_recv.at[i], sib).wait_recv()
+            h = hbuf[...].reshape(count * seq, width)
+            for c in range(2):
+                at = slice(c * features // 2, (c + 1) * features // 2)
+                tbuf[:count * seq, at] = dot_nn(h, vbuf[:, at]).astype(BF16)
+
+        pick(first, first_values)
         chunks = width // cw
 
         def chip_gap(index):
@@ -348,13 +358,20 @@
 
         def make_p(level, start, number):
             def chunk(j, _):
+                off = pl.multiple_of(j * cw, cw)
+                due = jnp.logical_and(j < chunks, chunk_level(jnp.minimum(j, chunks - 1)) == level)
+
                 def run():
-                    off = pl.multiple_of(j * cw, cw)
                     for m in range(nch):
                         block = dot_nt(vbuf[m * cn:(m + 1) * cn, :], wbuf[pl.ds(off, cw), :])
                         pbuf[m * cn:(m + 1) * cn, pl.ds(off, cw)] = block.astype(BF16)
 
-                pick(jnp.logical_and(j < chunks, chunk_level(jnp.minimum(j, chunks - 1)) == level), run)
+                def run_first():
+                    block = dot_nt(tbuf[:count * seq, :features], wbuf[pl.ds(off, cw), :])
+                    ubuf[:, :, pl.ds(off, cw)] = block.reshape(count, seq, cw)
+
+                pick(jnp.logical_and(due, sec > 0), run)
+                pick(jnp.logical_and(due, first), run_first)
                 return 0
 
             lax.fori_loop(start, start + number, chunk, 0)
@@ -396,30 +413,56 @@
         def whole(buf, mb, send, recv, dev):
             return remote(buf.at[mb], buf.at[mb], send.at[mb], recv.at[mb], dev)
 
+        def send_hidden(mb, lo, hi):
+            piece = pl.ds(lo, hi - lo)
+            remote(
+                obuf.at[mb, :, piece], hbuf.at[mb, :, piece], h_send.at[mb], h_recv.at[mb], nxt
+            ).start()
+
         def forward(mb, _):
-            pick(jnp.logical_or(sec > 0, mb < per), whole(hbuf, mb, h_send, h_recv, sib).wait_recv)
+            whole(hbuf, mb, h_send, h_recv, sib).wait_recv()
             h = hbuf[mb]
             h32 = h.astype(F32)
             r = inv_rms(h32)
             for lo, hi in zip(cuts, cuts[1:]):
-                piece = pl.ds(lo, hi - lo)
                 u = dot_tall(h, pbuf[:width, lo:hi])
                 ubuf[mb, :, lo:hi] = u
                 obuf[mb, :, lo:hi] = (h32[:, lo:hi] + r * u).astype(BF16)
-                remote(
-                    obuf.at[mb, :, piece], hbuf.at[mb, :, piece], h_send.at[mb], h_recv.at[mb], nxt
-                ).start()
+                send_hidden(mb, lo, hi)
             keep(hbuf, obuf, 0, mb).start()
             return 0
 
-        pick(sec < secs - 1, lambda: lax.fori_loop(0, count, forward, 0))
+        def forward_first(mb, _):
+            h32 = hbuf[mb].astype(F32)
+            obuf[mb] = (h32 + inv_rms(h32) * ubuf[mb]).astype(BF16)
+            for lo, hi in zip(cuts, cuts[1:]):
+                send_hidden(mb, lo, hi)
+            keep(hbuf, obuf, 0, mb).start()
+            return 0
+
+        pick(first, lambda: lax.fori_loop(0, count, forward_first, 0))
+        pick(
+            jnp.logical_and(sec > 0, sec < secs - 1),
+            lambda: lax.fori_loop(0, count, forward, 0),
+        )
         pick(jnp.logical_and(sec > 0, sec < tsec), make_t)
 
         def send_grad(mb, lo, hi):
             piece = pl.ds(lo, hi - lo)
-            remote(
-                qbuf.at[mb, :, piece], gbuf.at[mb, :, piece], g_send.at[mb], g_recv.at[mb], prv
-            ).start()
+
+            def to_relay():
+                remote(
+                    qbuf.at[mb, :, piece], gbuf.at[mb, :, piece], g_send.at[mb], g_recv.at[mb], prv
+                ).start()
+
+            def to_helper():
+                remote(
+                    qbuf.at[mb, :, piece], qbuf.at[mb, :, piece], g_send.at[mb], keep_recv.at[1, mb],
+                    (prv[0], prv[1] - 1),
+                ).start()
+
+            pick(sec != 1, to_relay)
+            pick(sec == 1, to_helper)
 
         def backward(batch, step, _):
             at = pl.ds(step * batch, batch)
@@ -460,11 +503,6 @@
                 send_grad(mb, lo, hi)
             return 0
 
-        def backward_first(mb, _):
-            whole(gbuf, mb, g_send, g_recv, sib).wait_recv()
-            keep(gbuf, qbuf, 1, mb).start()
-            return 0
-
         pick(last, lambda: lax.fori_loop(0, count, backward_last, 0))
         pick(
             jnp.logical_and(sec > 0, sec < secs - 2),
@@ -474,13 +512,12 @@
             jnp.logical_and(sec > 0, sec == secs - 2),
             lambda: lax.fori_loop(0, count // 2, functools.partial(backward, 2), 0),
         )
-        pick(first, lambda: lax.fori_loop(0, count, backward_first, 0))
 
         def drain(mb, _):
             pick(sec < secs - 1, whole(hbuf, mb, h_send, h_recv, nxt).wait_send)
             pick(sec > 0, whole(gbuf, mb, g_send, g_recv, prv).wait_send)
             keep(hbuf, obuf, 0, mb).wait_send()
-            keep(gbuf, qbuf, 1, mb).wait_send()
+            pick(sec > 0, keep(gbuf, qbuf, 1, mb).wait_send)
             return 0
 
         lax.fori_loop(0, count, drain, 0)

time: 244 us -> 236 us (0.967)
  Pallas kernels: 241 us -> 234 us
    pallas_call x1, Pallas kernels: 241 us -> 234 us  [per_device(): pl.pallas_call(functools.partial(relay_kernel, (secs, chips, per, width,...]
where the time goes in v4:
time: 236 us
  Pallas kernels  234 us (99%)
    pallas_call x1, Pallas kernels, per_device(): pl.pallas_call(functools.partial(relay_kernel, (secs, chips, per, width,...  234 us

profile of v4, /device:TPU:1, one launch (start us, length us, event | category | flops | bytes accessed | tf_op | source)
XLA Modules:
  0.0 235.6 jit_solution(16400619718008111569)
XLA Ops:
  0.0 233.7 %shard_map.55 = bf16[144,2048]{1,0:T(8,128)(2,1)} custom-call(bf16[4,32,2304]{2,1,0:T(8,128)(2,1)} %inp_ref.1, bf16[2304,2048]{1,0:T(8,128)(2,1)} %bitcast.3, bf16[144,2048]{1,0:T(8,128)(2,1)} %bitcast.5, bf16[4,32,2304]{2,1,0:T(8,128)(2,1)} %cot_ref.1, s32[4]{0:T(128)} %len_ref.1), custom_call_target="tpu_custom_call" | custom-call | tf_op jit(solution)/shard_map/pallas_call | solution.py:549
  233.7 1.9 copy.7

commit v5 on v4

--- a/solution.py
+++ b/solution.py
@@ -199,20 +199,22 @@
         def col_rows(mb):
             return pl.ds(pl.multiple_of(mb * seq, 16), seq)
 
-        def make_parts(mb, _):
-            keep(gbuf, qbuf, 1, mb).wait_recv()
-
+        def send_cols(mb):
             def to_owner(owner):
                 remote(
                     qbuf.at[mb, :, pl.ds(col_start(owner), span)], cols.at[chip, col_rows(mb), :],
                     col_send.at[owner], col_recv.at[chip], (sec, 2 * owner),
                 ).start()
 
+            others(chips, chip, to_owner)
+            cols[chip, col_rows(mb), :] = qbuf[mb, :, pl.ds(col_start(chip), span)]
+
+        def make_parts(mb, _):
+            keep(gbuf, qbuf, 1, mb).wait_recv()
             g = qbuf[mb]
             part = jnp.sum(grams[mb] * dot_nt(g, g), keepdims=True)
             parts[sec, pl.ds(mb, 1), :] = jnp.broadcast_to(part, (1, 128))
-            others(chips, chip, to_owner)
-            cols[chip, col_rows(mb), :] = qbuf[mb, :, pl.ds(col_start(chip), span)]
+            pick(mb < count - 1, lambda: send_cols(mb))
             return 0
 
         lax.fori_loop(0, count, make_parts, 0)
@@ -226,6 +228,11 @@
             )
 
         others(secs, sec, lambda to: part_copy(to, sec).start())
+        send_cols(count - 1)
+        others(secs, sec, lambda i: part_copy(i, i).wait_recv())
+        totals = jnp.sum(parts[...], axis=0)
+        scales[chip] = clip_scale / (jnp.sqrt(totals) + GAMMA)
+        others(chips, chip, lambda to: scale_copy(to, chip).start())
         block = count * seq
 
         def col_copy(owner, source):
@@ -238,10 +245,6 @@
             return 0
 
         lax.fori_loop(0, chips, turn, 0)
-        others(secs, sec, lambda i: part_copy(i, i).wait_recv())
-        totals = jnp.sum(parts[...], axis=0)
-        scales[chip] = clip_scale / (jnp.sqrt(totals) + GAMMA)
-        others(chips, chip, lambda to: scale_copy(to, chip).start())
         others(chips, chip, lambda i: scale_copy(i, i).wait_recv())
         lane = lax.broadcasted_iota(jnp.int32, (1, 128), 1)
         group = 128 // seq

time: 236 us -> 234 us (level)
  no operation moved by 1% of the time
where the time goes in v5:
time: 234 us
  Pallas kernels  232 us (99%)
    pallas_call x1, Pallas kernels, per_device(): pl.pallas_call(functools.partial(relay_kernel, (secs, chips, per, width,...  232 us

profile of v5, /device:TPU:1, one launch (start us, length us, event | category | flops | bytes accessed | tf_op | source)
XLA Modules:
  0.0 233.6 jit_solution(17751155767959089028)
XLA Ops:
  0.0 231.6 %shard_map.55 = bf16[144,2048]{1,0:T(8,128)(2,1)} custom-call(bf16[4,32,2304]{2,1,0:T(8,128)(2,1)} %inp_ref.1, bf16[2304,2048]{1,0:T(8,128)(2,1)} %bitcast.3, bf16[144,2048]{1,0:T(8,128)(2,1)} %bitcast.5, bf16[4,32,2304]{2,1,0:T(8,128)(2,1)} %cot_ref.1, s32[4]{0:T(128)} %len_ref.1), custom_call_target="tpu_custom_call" | custom-call | tf_op jit(solution)/shard_map/pallas_call | solution.py:552
  231.6 1.9 copy.7
